TPU v7x, 256 devices: a whole 4x4x8 slice. The times are simulated.
256 devices in a mesh: dp: 8 (over y_lo, x), space: 32 (over y_hi, z, core).
Axes of the slice: x: 4, y: 4 (y_hi: 2, y_lo: 2; y = y_hi * 2 + y_lo), z: 8, core: 2. Of those that a mesh axis runs over, the one named last changes fastest.
Arguments:
- fields: bfloat16 [8, 128, 48, 48, 128], P('dp', 'space'), may hold values from -6 to 6
- cotangent: bfloat16 [8, 128, 48, 48, 128], P('dp', 'space')
- neighbours: int32 [128, 4], replicated, may hold values from 0 to 127, as said below
- rotations: int32 [128, 4], replicated, may hold values from 0 to 3
- tile_counts: int32 [32], replicated, may hold values from 1 to 4, as said below
- depth_kernel: float32 [3, 3, 128], replicated, may hold values from -2 to 2
- depth_bias: float32 [128], replicated, may hold values from -3 to 3
- norm_gain: float32 [128], replicated, may hold values from 0.5 to 1.5
- norm_bias: float32 [128], replicated, may hold values from -3 to 3
- weight_in: bfloat16 [128, 512], replicated, may hold values from -0.5 to 0.5
- bias_in: float32 [512], replicated, may hold values from -3 to 3
- weight_out: bfloat16 [512, 128], replicated, may hold values from -0.25 to 0.25
- bias_out: float32 [128], replicated, may hold values from -3 to 3
- layer_scale: float32 [128], replicated, may hold values from 0.5 to 1.5
Outputs:
- blocks_out: bfloat16 [8, 128, 48, 48, 128], P('dp', 'space')
- grad_weight_in: float32 [128, 512], replicated
- grad_weight_out: float32 [512, 128], replicated
- grad_bias_in: float32 [512], replicated
- grad_channel: float32 [14, 128], replicated
Inputs may be any that keep to these rules, and one draw needn't show every extreme that they name: `neighbours`: every entry names a live slot. The 16 entries of the slots of one index of space name slots held by 16 different indices of space, so at most one line goes from one device to another. `tile_counts`: some index of space holds exactly 4 live tiles.
All inputs are finite; a program needn't handle non-finite values.
Results may differ from a plain program's by a relative error of at most 0.0065.
Values may be sent and summed in bfloat16 or wider, within the bound.
A program may use at most 128 MiB of HBM per device.

v0:
```python
import math

import jax
import jax.numpy as jnp
import numpy as np
from jax import lax
from jax.sharding import PartitionSpec as P


def side_pixels(width):
    grid = np.arange(width * width).reshape(width, width)
    table = np.zeros((4, 4, width), np.int32)
    turned = grid
    for turns in range(4):
        table[turns, 0] = turned[-1, :]
        table[turns, 1] = turned[:, 0]
        table[turns, 2] = turned[0, :]
        table[turns, 3] = turned[:, -1]
        turned = turned.T[::-1]
    return table


def border_places(width):
    pixels = side_pixels(width)
    rows = pixels // width
    cols = pixels % width
    places = np.where(
        rows == 0,
        cols,
        np.where(
            cols == width - 1,
            width + rows,
            np.where(rows == width - 1, 2 * width + cols, 3 * width + rows),
        ),
    )
    return places.astype(np.int32)


def framed_tiles(tiles, lines):
    lead = [(0, 0)] * (tiles.ndim - 3)
    padded = jnp.pad(tiles, lead + [(1, 1), (1, 1), (0, 0)])
    padded = padded.at[..., 0, 1:-1, :].set(lines[..., 0, :, :])
    padded = padded.at[..., 1:-1, -1, :].set(lines[..., 1, :, :])
    padded = padded.at[..., -1, 1:-1, :].set(lines[..., 2, :, :])
    padded = padded.at[..., 1:-1, 0, :].set(lines[..., 3, :, :])
    return padded


def tile_block(
    tiles,
    padded,
    live,
    cotan,
    depth_kernel,
    depth_bias,
    norm_gain,
    norm_bias,
    weight_in,
    bias_in,
    weight_out,
    bias_out,
    layer_scale,
):
    width = tiles.shape[-2]
    chans = tiles.shape[-1]
    conv = jnp.zeros(tiles.shape, jnp.float32) + depth_bias
    for row_off in range(3):
        for col_off in range(3):
            conv = (
                conv
                + padded[..., row_off : row_off + width, col_off : col_off + width, :].astype(
                    jnp.float32
                )
                * depth_kernel[row_off, col_off]
            )
    rows = conv.reshape(-1, chans)
    centre = rows - jnp.mean(rows, axis=-1, keepdims=True)
    inv_std = lax.rsqrt(jnp.mean(centre * centre, axis=-1, keepdims=True) + 1e-06)
    nhat = centre * inv_std
    normed = (nhat * norm_gain + norm_bias).astype(jnp.bfloat16)
    pre = jnp.dot(normed, weight_in, preferred_element_type=jnp.float32) + bias_in
    erf_part = jax.scipy.special.erf(pre * (1.0 / math.sqrt(2.0)))
    act = (0.5 * pre * (1.0 + erf_part)).astype(jnp.bfloat16)
    proj = jnp.dot(act, weight_out, preferred_element_type=jnp.float32) + bias_out
    keep = jnp.broadcast_to(live, tiles.shape[:-1] + (1,)).reshape(-1, 1)
    inputs = tiles.reshape(-1, chans).astype(jnp.float32)
    result = ((inputs + layer_scale * proj) * keep).astype(jnp.bfloat16).reshape(tiles.shape)
    grad_rows = cotan.reshape(-1, chans).astype(jnp.float32) * keep
    grad_scale = jnp.sum(grad_rows * proj, axis=0)
    branch_f = grad_rows * layer_scale
    grad_bout = jnp.sum(branch_f, axis=0)
    branch = branch_f.astype(jnp.bfloat16)
    contract_rows = (((0,), (0,)), ((), ()))
    contract_cols = (((1,), (1,)), ((), ()))
    grad_wout = lax.dot_general(act, branch, contract_rows, preferred_element_type=jnp.float32)
    dact = lax.dot_general(branch, weight_out, contract_cols, preferred_element_type=jnp.float32)
    slope = 0.5 * (1.0 + erf_part) + pre * jnp.exp(-0.5 * pre * pre) * (
        1.0 / math.sqrt(2.0 * math.pi)
    )
    dpre_f = dact * slope
    grad_bin = jnp.sum(dpre_f, axis=0)
    dpre = dpre_f.astype(jnp.bfloat16)
    grad_win = lax.dot_general(normed, dpre, contract_rows, preferred_element_type=jnp.float32)
    dnorm = lax.dot_general(dpre, weight_in, contract_cols, preferred_element_type=jnp.float32)
    grad_gain = jnp.sum(dnorm * nhat, axis=0)
    grad_nbias = jnp.sum(dnorm, axis=0)
    scaled = dnorm * norm_gain
    dconv = inv_std * (
        scaled
        - jnp.mean(scaled, axis=-1, keepdims=True)
        - nhat * jnp.mean(scaled * nhat, axis=-1, keepdims=True)
    )
    grad_dbias = jnp.sum(dconv, axis=0)
    dconv_tiles = dconv.reshape(tiles.shape)
    taps = []
    for row_off in range(3):
        for col_off in range(3):
            window = padded[..., row_off : row_off + width, col_off : col_off + width, :].astype(
                jnp.float32
            )
            taps.append(jnp.sum((dconv_tiles * window).reshape(-1, chans), axis=0))
    channel = jnp.stack(taps + [grad_dbias, grad_gain, grad_nbias, grad_bout, grad_scale], axis=0)
    return (result, grad_win, grad_wout, grad_bin, channel)


def local(
    fields,
    cotangent,
    neighbours,
    rotations,
    tile_counts,
    depth_kernel,
    depth_bias,
    norm_gain,
    norm_bias,
    weight_in,
    bias_in,
    weight_out,
    bias_out,
    layer_scale,
):
    slot_count = fields.shape[1]
    width = fields.shape[2]
    rank = lax.axis_index("space")
    places = jnp.asarray(border_places(width))
    border = jnp.concatenate(
        [
            fields[:, :, 0, :, :],
            fields[:, :, :, width - 1, :],
            fields[:, :, width - 1, :, :],
            fields[:, :, :, 0, :],
        ],
        axis=2,
    )
    my_nbrs = lax.dynamic_slice_in_dim(neighbours, rank * slot_count, slot_count, 0)
    my_turns = lax.dynamic_slice_in_dim(rotations, rank * slot_count, slot_count, 0)
    sides = jnp.arange(4, dtype=jnp.int32)[None, :]
    every_border = lax.all_gather(border, "space", axis=1, tiled=True)
    lines = every_border[:, my_nbrs[:, :, None], places[my_turns, sides]]
    padded = framed_tiles(fields, lines)
    slot_ids = jnp.arange(slot_count, dtype=jnp.int32)
    live = (slot_ids < tile_counts[rank]).astype(jnp.float32).reshape(1, slot_count, 1, 1, 1)
    result, grad_win, grad_wout, grad_bin, channel = tile_block(
        fields,
        padded,
        live,
        cotangent,
        depth_kernel,
        depth_bias,
        norm_gain,
        norm_bias,
        weight_in,
        bias_in,
        weight_out,
        bias_out,
        layer_scale,
    )
    grad_win, grad_wout, grad_bin, channel = lax.psum(
        (grad_win, grad_wout, grad_bin, channel), ("dp", "space")
    )
    return (result, grad_win, grad_wout, grad_bin, channel)


def solution(mesh):
    return jax.shard_map(
        local,
        mesh=mesh,
        in_specs=(
            P("dp", "space", None, None, None),
            P("dp", "space", None, None, None),
            P(),
            P(),
            P(),
            P(),
            P(),
            P(),
            P(),
            P(),
            P(),
            P(),
            P(),
            P(),
        ),
        out_specs=(P("dp", "space", None, None, None), P(), P(), P(), P()),
        check_vma=False,
    )
```

profile of v0, /device:TPU:1, one launch (start us, length us, event | category | flops | bytes accessed | tf_op | source)
XLA Modules:
  0.0 449.0 jit_solution(11106188503417843805)
XLA Ops:
  7.2 0.8 slice_bitcast_fusion.3
  8.1 1.3 fusion.41
  9.4 0.7 pad_maximum_fusion
  10.2 0.8 fusion.35
  11.2 1.3 gather_fusion
  12.7 1.2 dynamic_slice.11
  13.9 0.6 compare_convert_fusion
  14.8 3.0 pad.20
  17.8 0.6 fusion.42
  18.4 1.5 multiply_reduce_fusion.1
  19.9 90.3 %all-gather.2.cloned.1.call-done = bf16[1,128,192,128]{3,2,0,1:T(8,128)(2,1)} async-done(((bf16[1,4,192,128]{3,2,0,1:T(8,128)(2,1)}), bf16[1,128,192,128]{3,2,0,1:T(8,128)(2,1)}) %all-gather.2.cloned.1.call-update) | async-done | bytes 6291472 | tf_op jit(solution)/shard_map/all_gather | solution.py:158
  110.1 7.6 %gather_fusion.1 = bf16[768,128]{1,0:T(8,128)(2,1)S(1)} fusion(bf16[128,192,128]{2,1,0:T(8,128)(2,1)} %bitcast.91, s32[768]{0:T(1024)S(1)} %reshape.353), kind=kCustom, calls=%fused_computation.1 | custom fusion | bytes 399360 | tf_op jit(solution)/shard_map/gather | solution.py:159
  117.9 1.6 scatter.14
  119.5 2.0 scatter.15
  121.5 0.3 scatter.16
  121.8 2.0 scatter.19
  123.8 6.7 %fusion.39 = (f32[4,48,48]{2,1,0:T(8,128)S(1)}, f32[1,4,48,48,128]{4,3,2,1,0:T(8,128)}) fusion(f32[128]{0:T(128)S(1)} %get-tuple-element.92, bf16[1,4,50,50,128]{4,3,2,1,0:T(8,128)(2,1)S(1)} %scatter.19, f32[128]{0:T(128)S(1)} %get-tuple-element.93, f32[128]{0:T(128)S(1)} %get-tuple-element.86, f32[128]{0:T(128)S(1)} %get-tuple-element.87, ...), kind=kLoop, calls=%fused_computation.100 | loop fusion | flops 33020928 | bytes 25994240 | tf_op jit(solution)/shard_map/reduce_sum | solution.py:77
  130.6 4.6 %multiply_reduce_fusion.4 = f32[4,48,48]{2,1,0:T(8,128)S(1)} fusion(f32[1,4,48,48,128]{4,3,2,1,0:T(8,128)} %get-tuple-element.73, f32[4,48,48]{2,1,0:T(8,128)S(1)} %broadcast_multiply_fusion), kind=kLoop, calls=%fused_computation.64 | loop fusion | flops 3529728 | bytes 4792320 | tf_op jit(solution)/shard_map/reduce_sum | solution.py:78
  135.4 6.8 %fusion.25 = f32[9216,128]{1,0:T(8,128)S(1)} fusion(f32[1,4,48,48,128]{4,3,2,1,0:T(8,128)} %get-tuple-element.73, f32[9216]{0:T(1024)S(1)} %rsqrt.12, f32[9216]{0:T(1024)S(1)} %div.15), kind=kLoop, calls=%fused_computation.52 | loop fusion | flops 2359296 | bytes 9510912 | tf_op jit(solution)/shard_map/mul | solution.py:79
  142.3 10.6 %multiply_convert_fusion = (bf16[9216,512]{1,0:T(8,128)(2,1)S(1)}, f32[9216,512]{1,0:T(8,128)}) fusion(f32[512]{0:T(512)S(1)} %copy-done.7, bf16[128,512]{1,0:T(8,128)(2,1)S(1)} %copy-done, f32[9216,128]{1,0:T(8,128)S(1)} %fusion.25, f32[128]{0:T(128)S(1)} %copy-done.8, f32[128]{0:T(128)S(1)} %copy-done.6), kind=kOutput, calls=%fused_computation.8 | convolution fusion | flops 1239810048 | bytes 33164288 | tf_op jit(solution)/shard_map/dot_general | solution.py:81
  153.0 5.1 %multiply_reduce_fusion = (f32[128]{0:T(128)S(1)}, bf16[9216,128]{1,0:T(8,128)(2,1)}, bf16[9216,128]{1,0:T(8,128)(2,1)S(1)}) fusion(bf16[1,4,48,48,128]{4,3,2,1,0:T(8,128)(2,1)S(1)} %copy-done.5, f32[9216]{0:T(1024)S(1)} %broadcast_in_dim.14, f32[128]{0:T(128)S(1)} %copy-done.11, bf16[1,4,48,48,128]{4,3,2,1,0:T(8,128)(2,1)S(1)} %copy-done.3, ...), kind=kOutput, calls=%fused_computation.53 | convolution fusion | flops 1222115200 | bytes 19043840 | tf_op jit(solution)/shard_map/dot_general | solution.py:84
  158.1 3.3 fusion.44
  161.4 14.1 %fusion.43 = (f32[512]{0:T(512)S(1)}, bf16[9216,512]{1,0:T(8,128)(2,1)S(1)}) fusion(f32[9216,512]{1,0:T(8,128)} %get-tuple-element.97, f32[512]{0:T(512)S(1)} %copy-done.7, bf16[9216,128]{1,0:T(8,128)(2,1)S(1)} %get-tuple-element.76, bf16[512,128]{1,0:T(8,128)(2,1)S(1)} %copy-done.12), kind=kOutput, calls=%fused_computation.103 | convolution fusion | flops 1264582144 | bytes 30806016 | tf_op jit(solution)/shard_map/dot_general | solution.py:96
  175.5 3.6 copy-done.2
  179.1 2.2 fusion.28
  181.3 9.9 %multiply_reduce_fusion.2 = (f32[128]{0:T(128)S(1)}, f32[9216]{0:T(1024)S(1)}, f32[9216]{0:T(1024)S(1)}, f32[128]{0:T(128)S(1)}, f32[9216,128]{1,0:T(8,128)}) fusion(f32[9216,128]{1,0:T(8,128)} %copy-done.1, f32[128]{0:T(128)S(1)} %copy-done.6, bf16[128,512]{1,0:T(8,128)(2,1)S(1)} %copy-done, bf16[9216,512]{1,0:T(8,128)(2,1)} %copy-done.2), kind=kOutput, calls=%fused_computation.55 | convolution fusion | flops 1216198400 | bytes 19080704 | tf_op jit(solution)/shard_map/dot_general | solution.py:104
  191.3 7.9 %fusion.38 = (f32[128]{0:T(128)S(1)}, f32[9216,128]{1,0:T(8,128)S(1)}) fusion(f32[9216]{0:T(1024)S(1)} %broadcast_multiply_fusion.1, f32[9216]{0:T(1024)S(1)} %broadcast_multiply_fusion.2, f32[9216,128]{1,0:T(8,128)} %get-tuple-element.100, f32[128]{0:T(128)S(1)} %copy-done.6, f32[9216]{0:T(1024)S(1)} %rsqrt.12, f32[9216]{0:T(1024)S(1)} %div.15, ...), kind=kLoop, calls=%fused_computation.99 | loop fusion | flops 9437056 | bytes 14304256 | tf_op jit(solution)/shard_map/reduce_sum | solution.py:113
  199.2 5.8 %fusion.22 = (f32[128]{0:T(128)S(1)}, f32[128]{0:T(128)S(1)}, f32[128]{0:T(128)S(1)}, f32[128]{0:T(128)S(1)}, f32[128]{0:T(128)S(1)}, /*index=5*/f32[128]{0:T(12...) fusion(f32[1,4,48,48,128]{4,3,2,1,0:T(8,128)S(1)} %bitcast.89, bf16[1,4,50,50,128]{4,3,2,1,0:T(8,128)(2,1)S(1)} %scatter.19), kind=kLoop, calls=%fused_computation.46 | loop fusion | flops 31849344 | bytes 25956864 | tf_op jit(solution)/shard_map/reduce_sum | solution.py:121
  205.1 75.4 %all-reduce.1 = (f32[512]{0:T(512)}, f32[14,128]{1,0:T(8,128)}) all-reduce(f32[512]{0:T(512)S(1)} %get-tuple-element.98, f32[14,128]{1,0:T(8,128)S(1)} %stack.59), channel_id=1, replica_groups=mesh['dp'=8,'space'=32] {'dp','space'}, use_global_device_ids=true, to_apply=%region_5.6 | all-reduce | flops 2304 | bytes 18432 | tf_op jit(solution)/shard_map/psum | solution.py:178
  280.5 158.3 %all-reduce.5.cloned.1.call-done = (f32[128,512]{1,0:T(8,128)}, f32[512,128]{1,0:T(8,128)}) async-done(((f32[128,512]{1,0:T(8,128)}, f32[512,128]{1,0:T(8,128)}), (f32[128,512]{1,0:T(8,128)}, f32[512,128]{1,0:T(8,128)})) %all-reduce.5.cloned.1.call-update) | async-done | bytes 524304 | tf_op jit(solution)/shard_map/psum | solution.py:178
  438.8 1.7 copy.59
  440.5 1.7 copy.60
  (52 shorter events, 1.3 us)
Async XLA Ops:
  7.2 135.1 %copy-start = (bf16[128,512]{1,0:T(8,128)(2,1)S(1)}, bf16[128,512]{1,0:T(8,128)(2,1)}, u32[]{:S(2)}) copy-start(bf16[128,512]{1,0:T(8,128)(2,1)} %param.32) | copy-start | bytes 393220
  7.2 11.2 %copy-start.9 = (f32[3,3,128]{2,1,0:T(4,128)S(1)}, f32[3,3,128]{2,1,0:T(4,128)}, u32[]{:S(2)}) copy-start(f32[3,3,128]{2,1,0:T(4,128)} %param.28) | copy-start | bytes 13828
  7.2 11.2 %copy-start.11 = (f32[128]{0:T(128)S(1)}, f32[128]{0:T(128)}, u32[]{:S(2)}) copy-start(f32[128]{0:T(128)} %param.36) | copy-start | bytes 1540
  7.2 102.9 %all-gather.2.cloned.1.call-start = ((), (), s32[]{:S(2)}) async-start(), calls=%async_computation | async-start | bytes 6488064 | tf_op jit(solution)/shard_map/all_gather | solution.py:158
  10.1 428.7 %all-reduce.5.cloned.1.call-start = ((), (), s32[]{:S(2)}) async-start(), calls=%async_computation.1 | async-start | bytes 1048576 | tf_op jit(solution)/shard_map/psum | solution.py:178
  14.8 3.6 copy-start.4
  14.8 109.0 %copy-start.10 = (f32[128]{0:T(128)S(1)}, f32[128]{0:T(128)}, u32[]{:S(2)}) copy-start(f32[128]{0:T(128)} %param.29) | copy-start | bytes 1540
  135.4 6.9 %copy-start.6 = (f32[128]{0:T(128)S(1)}, f32[128]{0:T(128)}, u32[]{:S(2)}) copy-start(f32[128]{0:T(128)} %param.30) | copy-start | bytes 1540
  135.4 6.9 %copy-start.7 = (f32[512]{0:T(512)S(1)}, f32[512]{0:T(512)}, u32[]{:S(2)}) copy-start(f32[512]{0:T(512)} %param.33) | copy-start | bytes 6148
  135.4 6.9 %copy-start.8 = (f32[128]{0:T(128)S(1)}, f32[128]{0:T(128)}, u32[]{:S(2)}) copy-start(f32[128]{0:T(128)} %param.31) | copy-start | bytes 1540
  142.3 33.2 %copy-start.1 = (f32[9216,128]{1,0:T(8,128)}, f32[9216,128]{1,0:T(8,128)S(1)}, u32[]{:S(2)}) copy-start(f32[9216,128]{1,0:T(8,128)S(1)} %fusion.25) | copy-start | bytes 14155780
  142.3 10.6 %copy-start.3 = (bf16[1,4,48,48,128]{4,3,2,1,0:T(8,128)(2,1)S(1)}, bf16[1,4,48,48,128]{4,3,2,1,0:T(8,128)(2,1)}, u32[]{:S(2)}) copy-start(bf16[1,4,48,48,128]{4,3,2,1,0:T(8,128)(2,1)} %param.23) | copy-start | bytes 7077892
  142.3 10.6 %copy-start.5 = (bf16[1,4,48,48,128]{4,3,2,1,0:T(8,128)(2,1)S(1)}, bf16[1,4,48,48,128]{4,3,2,1,0:T(8,128)(2,1)}, u32[]{:S(2)}) copy-start(bf16[1,4,48,48,128]{4,3,2,1,0:T(8,128)(2,1)} %param.24) | copy-start | bytes 7077892
  142.3 10.6 %copy-start.12 = (bf16[512,128]{1,0:T(8,128)(2,1)S(1)}, bf16[512,128]{1,0:T(8,128)(2,1)}, u32[]{:S(2)}) copy-start(bf16[512,128]{1,0:T(8,128)(2,1)} %param.34) | copy-start | bytes 393220
  142.3 10.6 %copy-start.13 = (f32[128]{0:T(128)S(1)}, f32[128]{0:T(128)}, u32[]{:S(2)}) copy-start(f32[128]{0:T(128)} %param.35) | copy-start | bytes 1540
  175.5 3.6 copy-start.2
Sparse Core Ops, SparseCore 0:
  11.4 98.7 all-gather.1
  191.4 247.3 all-reduce.4
where the time goes:
time: 450 us; the launch traced here: 449 us
  waiting for transfers between devices  249 us (55%)
  blocking collectives  75.4 us (17%)
  matrix products  45.3 us (10%)
  other arithmetic  35.6 us (8%)
  local copies, waits for them, and re-layouts  29.7 us (7%)
  between operations  14.4 us (3%)
    psum x1, waiting for transfers between devices, local(): lax.psum((grad_win, grad_wout, grad_bin, channel), ('dp', 'space'))  158 us
    all_gather x1, waiting for transfers between devices, local(): every_border = lax.all_gather(border, 'space', axis=1, tiled=True)  90.3 us
    psum x1, blocking collectives, local(): lax.psum((grad_win, grad_wout, grad_bin, channel), ('dp', 'space'))  75.4 us
    dot_general x1, matrix products, tile_block(): lax.dot_general(branch, weight_out, contract_cols, preferred_element_type...  14.1 us
    dot_general x1, matrix products, tile_block(): jnp.dot(normed, weight_in, preferred_element_type=jnp.float32) + bias_in  10.6 us
    dot_general x1, matrix products, tile_block(): lax.dot_general(dpre, weight_in, contract_cols, preferred_element_type=jn...  9.94 us
  transfers between devices with their start and end apart: 2, of which 2 were waited for; matrix products, arithmetic and copies ran while one was open for 5% of the time, Pallas kernels for 0%

commit v1 on v0

v1 whole, which is shorter than its diff:
```python
import functools
import math

import jax
import jax.numpy as jnp
from jax import lax
from jax.experimental import pallas as pl
from jax.experimental.pallas import tpu as pltpu
from jax.sharding import PartitionSpec as P

F32, BF16 = jnp.float32, jnp.bfloat16
PITCH = 64
ROWS = 16
GROUP = 64
HALF = 256
def over_rows(a):
    return jnp.sum(a.reshape(-1, 8, a.shape[-1]), axis=0)

def contract_rows(a, b):
    return lax.dot_general(a, b, (((0,), (0,)), ((), ())), preferred_element_type=F32)

def block_kernel(count, tile, cotan, lines, taps_w, dbias, gain, nbias, win, bin_, wout, bout, scale,
                 out, grads, small, frame, win_t, wout_t, nhat_s, normed_s, branch_s, act_s, dpre_s, dconv_s, sums, bsum):
    t = pl.program_id(0)
    width, chans = tile.shape[1], tile.shape[2]
    hid = win.shape[1]

    @pl.when(t == 0)
    def _():
        win_t[...] = win[...].T
        wout_t[...] = wout[...].T
        grads[...] = jnp.zeros_like(grads)
        sums[...] = jnp.zeros_like(sums)
        bsum[...] = jnp.zeros_like(bsum)
        frame[...] = jnp.zeros_like(frame)

    @pl.when(t >= count[0])
    def _():
        out[...] = jnp.zeros_like(out)

    @pl.when(t < count[0])
    def _():
        def fill(r, c):
            frame[pl.ds(pl.multiple_of((r + 1) * PITCH + 8, 8), width), :] = tile[r].astype(F32)
            return c
        lax.fori_loop(0, width, fill, 0, unroll=4)
        frame[pl.ds(8, width), :] = lines[0].astype(F32)
        frame[pl.ds((width + 1) * PITCH + 8, width), :] = lines[2].astype(F32)
        frame[pl.ds(PITCH + 8 + width, width, stride=PITCH), :] = lines[1].astype(F32)
        frame[pl.ds(PITCH + 7, width, stride=PITCH), :] = lines[3].astype(F32)

        def chunk(c, carry):
            top = c * ROWS
            rows = ROWS * width
            kern = [[taps_w[3 * a + b] for b in range(3)] for a in range(3)]
            bias = dbias[...]
            inv = []
            conv = {}
            for fr in range(ROWS + 2):
                base = (top + fr) * PITCH + 7
                win3 = [frame[pl.ds(base + b, width), :] for b in range(3)]
                for a in range(3):
                    r = fr - a
                    if 0 <= r < ROWS:
                        acc = conv.get(r, bias)
                        for b in range(3):
                            acc = acc + win3[b] * kern[a][b]
                        conv[r] = acc
                r = fr - 2
                if r >= 0:
                    x = conv.pop(r)
                    x = x - jnp.mean(x, axis=-1, keepdims=True)
                    iv = lax.rsqrt(jnp.mean(x * x, axis=-1, keepdims=True) + 1e-06)
                    nhat = x * iv
                    inv.append(iv)
                    sl = pl.ds(r * width, width)
                    nhat_s[sl, :] = nhat
                    normed_s[sl, :] = (nhat * gain[...] + nbias[...]).astype(BF16)
                    g = cotan[top + r].astype(F32)
                    branch_s[sl, :] = (g * scale[...]).astype(BF16)
            normed = normed_s[...]
            branch = branch_s[...]
            for h in range(0, hid, HALF):
                hs = pl.ds(h, HALF)
                pre_h = jnp.dot(normed, win[:, hs], preferred_element_type=F32)
                dact_h = jnp.dot(branch, wout_t[:, hs], preferred_element_type=F32)
                bs = jnp.zeros((8, HALF), F32)
                for q in range(0, rows, GROUP):
                    pre = pre_h[q:q + GROUP] + bin_[:, hs]
                    ph = 0.5 * lax.erf(pre * (1.0 / math.sqrt(2.0))) + 0.5
                    act_s[pl.ds(q, GROUP), hs] = (pre * ph).astype(BF16)
                    slope = ph + pre * (jnp.exp(-0.5 * pre * pre) * (1.0 / math.sqrt(2.0 * math.pi)))
                    dpre = dact_h[q:q + GROUP] * slope
                    bs = bs + over_rows(dpre)
                    dpre_s[pl.ds(q, GROUP), hs] = dpre.astype(BF16)
                bsum[:, hs] += bs
            act = act_s[...]
            dpre = dpre_s[...]
            grads[0:chans, :] += contract_rows(normed, dpre)
            grads[chans:2 * chans, :] += contract_rows(branch, act)
            proj_a = jnp.dot(act, wout[...], preferred_element_type=F32)
            dnorm_a = jnp.dot(dpre, win_t[...], preferred_element_type=F32)
            s_g = s_gp = s_dn = s_dnh = s_dc = jnp.zeros((8, chans), F32)
            for r in range(ROWS):
                sl = slice(r * width, (r + 1) * width)
                proj = proj_a[sl]
                x = tile[top + r].astype(F32)
                out[top + r] = (x + scale[...] * (proj + bout[...])).astype(BF16)
                g = cotan[top + r].astype(F32)
                s_g = s_g + over_rows(g)
                s_gp = s_gp + over_rows(g * proj)
                dnorm = dnorm_a[sl]
                nhat = nhat_s[pl.ds(r * width, width), :]
                dnh = dnorm * nhat
                s_dn = s_dn + over_rows(dnorm)
                s_dnh = s_dnh + over_rows(dnh)
                m1 = jnp.mean(dnorm * gain[...], axis=-1, keepdims=True)
                m2 = jnp.mean(dnh * gain[...], axis=-1, keepdims=True)
                dconv = inv[r] * (dnorm * gain[...] - m1 - nhat * m2)
                s_dc = s_dc + over_rows(dconv)
                dconv_s[pl.ds(r * width, width), :] = dconv
            taps = [[jnp.zeros((8, chans), F32)] * 3 for _ in range(3)]
            for fr in range(ROWS + 2):
                base = (top + fr) * PITCH + 7
                win3 = [frame[pl.ds(base + b, width), :] for b in range(3)]
                for a in range(3):
                    r = fr - a
                    if 0 <= r < ROWS:
                        d = dconv_s[pl.ds(r * width, width), :]
                        for b in range(3):
                            taps[a][b] = taps[a][b] + over_rows(d * win3[b])
            for i, s in enumerate([taps[a][b] for a in range(3) for b in range(3)] + [s_dc, s_dnh, s_dn, s_g, s_gp]):
                sums[i] += s
            return carry
        lax.fori_loop(0, width // ROWS, chunk, 0)

    @pl.when(t == pl.num_programs(0) - 1)
    def _():
        tot = jnp.sum(sums[...], axis=1)
        small[...] = jnp.zeros_like(small)
        small[0:12, :] = tot[0:12]
        small[12:13, :] = tot[12:13] * scale[...]
        small[13:14, :] = tot[13:14] + tot[12:13] * bout[...]
        b = jnp.sum(bsum[...], axis=0, keepdims=True)
        for i in range(hid // chans):
            small[14 + i:15 + i, :] = b[:, i * chans:(i + 1) * chans]

def block(count, fields, cotan, lines, kern, dbias, gain, nbias, win, bin_, wout, bout, scale):
    slots, width, _, chans = fields.shape
    hid = win.shape[1]
    m = ROWS * width
    row = lambda v: v.reshape(1, -1)
    full = lambda *s: pl.BlockSpec(s, lambda t: (0,) * len(s))
    tiles = pl.BlockSpec((None, width, width, chans), lambda t: (t, 0, 0, 0))
    vec = full(1, chans)
    return pl.pallas_call(
        block_kernel,
        grid=(slots,),
        in_specs=[pl.BlockSpec(memory_space=pltpu.SMEM), tiles, tiles,
                  pl.BlockSpec((None, 4, width, chans), lambda t: (t, 0, 0, 0)),
                  full(9, 1, chans), vec, vec, vec, full(chans, hid), full(1, hid), full(hid, chans), vec, vec],
        out_specs=[tiles, full(2 * chans, hid), full(24, chans)],
        out_shape=[jax.ShapeDtypeStruct(fields.shape, BF16), jax.ShapeDtypeStruct((2 * chans, hid), F32),
                   jax.ShapeDtypeStruct((24, chans), F32)],
        scratch_shapes=[
            pltpu.VMEM(((width + 2) * PITCH + 8, chans), F32),
            pltpu.VMEM((hid, chans), BF16), pltpu.VMEM((chans, hid), BF16),
            pltpu.VMEM((m, chans), F32), pltpu.VMEM((m, chans), BF16), pltpu.VMEM((m, chans), BF16),
            pltpu.VMEM((m, hid), BF16), pltpu.VMEM((m, hid), BF16), pltpu.VMEM((m, chans), F32),
            pltpu.VMEM((14, 8, chans), F32), pltpu.VMEM((8, hid), F32)],
        compiler_params=pltpu.CompilerParams(vmem_limit_bytes=56 * 2**20),
    )(count, fields, cotan, lines, kern.reshape(9, 1, chans), row(dbias), row(gain), row(nbias), win, row(bin_), wout, row(bout), row(scale))


MESH = pl.DeviceIdType.MESH


def remote(src, dst, send_sem, recv_sem, device):
    return pltpu.make_async_remote_copy(
        src_ref=src, dst_ref=dst, send_sem=send_sem, recv_sem=recv_sem, device_id=device, device_id_type=MESH
    )


def halo_kernel(space, nbrs, turns, edges, lines, cand, outgo, income, send_sem, recv_sem):
    dp, me = lax.axis_index("dp"), lax.axis_index("space")
    slots, width = edges.shape[1], edges.shape[2]
    picks = 4 * slots
    barrier = pltpu.get_barrier_semaphore()

    def greet(o, c):
        pl.semaphore_signal(barrier, inc=1, device_id=(dp, lax.rem(me + o, space)), device_id_type=MESH)
        return c

    lax.fori_loop(1, space, greet, 0)
    i = lax.broadcasted_iota(jnp.int32, (width, width), 0)
    j = lax.broadcasted_iota(jnp.int32, (width, width), 1)
    mirror = (i + j == width - 1).astype(BF16)

    def candidates(k, c):
        for q in range(4):
            line = edges[q, k]
            cand[4 * k + q] = line
            cand[picks + 4 * k + q] = jnp.dot(mirror, line, preferred_element_type=F32).astype(BF16)
        return c

    lax.fori_loop(0, slots, candidates, 0)

    def pick(o, c):
        peer = lax.rem(me + o, space)
        code = jnp.int32(0)
        for k in range(picks):
            slot, side = peer * slots + k // 4, k % 4
            nbr, turn = nbrs[slot, side], turns[slot, side]
            edge = (turn + (side + 2)) & 3
            flip = ((turn + (side & 1)) >> 1) & 1
            mine = flip * picks + 4 * (nbr & (slots - 1)) + edge
            code = jnp.where(nbr // slots == me, mine, code)
        outgo[o] = cand[code]
        return c

    lax.fori_loop(0, space, pick, 0)
    income[me] = outgo[0]
    pl.semaphore_wait(barrier, space - 1)

    def send(o, c):
        remote(outgo.at[o], income.at[me], send_sem.at[o], recv_sem.at[me], (dp, lax.rem(me + o, space))).start()
        return c

    def settle(o, c):
        src = lax.rem(me + space - o, space)
        remote(outgo.at[o], income.at[src], send_sem.at[o], recv_sem.at[src], (dp, src)).wait()
        return c

    lax.fori_loop(1, space, send, 0)
    lax.fori_loop(1, space, settle, 0)
    for k in range(picks):
        lines[k // 4, k % 4] = income[nbrs[me * slots + k // 4, k % 4] // slots]


def halo(space, nbrs, turns, edges):
    _, slots, width, chans = edges.shape
    line = (width, chans)
    smem, vmem = pl.BlockSpec(memory_space=pltpu.SMEM), pl.BlockSpec(memory_space=pltpu.VMEM)
    return pl.pallas_call(
        functools.partial(halo_kernel, space),
        in_specs=[smem, smem, vmem],
        out_specs=vmem,
        out_shape=jax.ShapeDtypeStruct((slots, 4) + line, BF16),
        scratch_shapes=[
            pltpu.VMEM((8 * slots,) + line, BF16),
            pltpu.VMEM((space,) + line, BF16),
            pltpu.VMEM((space,) + line, BF16),
            pltpu.SemaphoreType.DMA((space,)),
            pltpu.SemaphoreType.DMA((space,)),
        ],
        compiler_params=pltpu.CompilerParams(collective_id=0, has_side_effects=True, vmem_limit_bytes=32 * 2**20),
    )(nbrs, turns, edges)


def reduce_kernel(near, far, ring, grads, small, whole, small_out, halves, got, small_got, tiles, small_mid,
                  far_got, small_far, final, spread, sems_a, sems_b, sems_c, sems_d, sems_e, sems_f):
    dp, space = lax.axis_index("dp"), lax.axis_index("space")
    core, plane = lax.rem(space, 2), space // 2
    a, b = dp * 2 + core, plane
    z, base = lax.rem(plane, ring), (plane // ring) * ring
    rows, cols = whole.shape[1], whole.shape[2]

    def near_id(o):
        p = lax.rem(a + o, near)
        return p, (p // 2, plane * 2 + lax.rem(p, 2))

    def far_id(o):
        p = lax.rem(b + o, far)
        return p, (dp, p * 2 + core)

    def ring_id(o):
        p = lax.rem(z + o, ring)
        return p, (dp, (base + p) * 2 + core)

    barrier = pltpu.get_barrier_semaphore()

    def greet_near(o, c):
        pl.semaphore_signal(barrier, inc=1, device_id=near_id(o)[1], device_id_type=MESH)
        return c

    def greet_far(o, c):
        pl.semaphore_signal(barrier, inc=1, device_id=far_id(o)[1], device_id_type=MESH)
        return c

    lax.fori_loop(1, near, greet_near, 0)
    lax.fori_loop(1, far, greet_far, 0)
    for p in range(near):
        halves[p] = grads[pl.ds(p * rows, rows), :].astype(BF16)
    pl.semaphore_wait(barrier, near + far - 2)

    def send_near(o, c):
        p, device = near_id(o)
        remote(halves.at[p], got.at[a], sems_a.at[0, o], sems_a.at[1, a], device).start()
        remote(small, small_got.at[a], sems_b.at[0, o], sems_b.at[1, a], device).start()
        return c

    def settle_near(o, c):
        p, device = near_id(near - o)
        remote(halves.at[p], got.at[p], sems_a.at[0, o], sems_a.at[1, p], device).wait()
        remote(small, small_got.at[p], sems_b.at[0, o], sems_b.at[1, p], device).wait()
        return c

    lax.fori_loop(1, near, send_near, 0)
    got[a] = halves[a]
    small_got[a] = small[...]
    lax.fori_loop(1, near, settle_near, 0)
    tot = got[0].astype(F32)
    s = small_got[0]
    for p in range(1, near):
        tot = tot + got[p].astype(F32)
        s = s + small_got[p]
    per = cols // 128
    for p in range(ring):
        r, q = p // per, p % per
        tiles[p] = tot[r * 8:r * 8 + 8, q * 128:q * 128 + 128]
    small_mid[...] = s

    def send_far(o, c):
        p, device = far_id(o)
        remote(tiles.at[lax.rem(p, ring)], far_got.at[b], sems_c.at[0, o], sems_c.at[1, b], device).start()
        remote(small_mid, small_far.at[b], sems_d.at[0, o], sems_d.at[1, b], device).start()
        return c

    def settle_far(o, c):
        p, device = far_id(far - o)
        remote(tiles.at[lax.rem(p, ring)], far_got.at[p], sems_c.at[0, o], sems_c.at[1, p], device).wait()
        remote(small_mid, small_far.at[p], sems_d.at[0, o], sems_d.at[1, p], device).wait()
        return c

    lax.fori_loop(1, far, send_far, 0)
    far_got[b] = tiles[z]
    small_far[b] = s
    lax.fori_loop(1, far, settle_far, 0)
    t = far_got[0]
    s = small_far[0]
    for p in range(1, far):
        t = t + far_got[p]
        s = s + small_far[p]
    small_out[...] = s
    final[z] = t

    def send_ring(o, c):
        p, device = ring_id(o)
        remote(final.at[z], final.at[z], sems_e.at[0, o], sems_e.at[1, z], device).start()
        return c

    def settle_ring(o, c):
        p, device = ring_id(ring - o)
        remote(final.at[z], final.at[p], sems_e.at[0, o], sems_e.at[1, p], device).wait()
        return c

    lax.fori_loop(1, ring, send_ring, 0)
    lax.fori_loop(1, ring, settle_ring, 0)
    for q in range(per):
        spread[:, q * 128:(q + 1) * 128] = jnp.concatenate([final[q], final[per + q]], axis=0).astype(BF16)

    def send_back(o, c):
        p, device = near_id(o)
        remote(spread, whole.at[a], sems_f.at[0, o], sems_f.at[1, a], device).start()
        return c

    def settle_back(o, c):
        p, device = near_id(near - o)
        remote(spread, whole.at[p], sems_f.at[0, o], sems_f.at[1, p], device).wait()
        return c

    lax.fori_loop(1, near, send_back, 0)
    whole[a] = spread[...]
    lax.fori_loop(1, near, settle_back, 0)


def reduce_all(near, far, ring, grads, small):
    rows, cols = grads.shape[0] // near, grads.shape[1]
    vmem = pl.BlockSpec(memory_space=pltpu.VMEM)
    sems = lambda n: pltpu.SemaphoreType.DMA((2, n))
    return pl.pallas_call(
        functools.partial(reduce_kernel, near, far, ring),
        in_specs=[vmem, vmem],
        out_specs=[vmem, vmem],
        out_shape=[jax.ShapeDtypeStruct((near, rows, cols), BF16), jax.ShapeDtypeStruct(small.shape, F32)],
        scratch_shapes=[
            pltpu.VMEM((near, rows, cols), BF16),
            pltpu.VMEM((near, rows, cols), BF16),
            pltpu.VMEM((near,) + small.shape, F32),
            pltpu.VMEM((ring, 8, 128), F32),
            pltpu.VMEM(small.shape, F32),
            pltpu.VMEM((far, 8, 128), F32),
            pltpu.VMEM((far,) + small.shape, F32),
            pltpu.VMEM((ring, 8, 128), F32),
            pltpu.VMEM((rows, cols), BF16),
            sems(near), sems(near), sems(far), sems(far), sems(ring), sems(near),
        ],
        compiler_params=pltpu.CompilerParams(collective_id=1, has_side_effects=True, vmem_limit_bytes=32 * 2**20),
    )(grads, small)


def local(fields, cotangent, neighbours, rotations, tile_counts, depth_kernel, depth_bias, norm_gain, norm_bias,
          weight_in, bias_in, weight_out, bias_out, layer_scale, shape):
    tiles, cotan = fields[0], cotangent[0]
    width = tiles.shape[1]
    chans, hid = weight_in.shape
    space, near = shape["space"], 2 * shape["dp"]
    far = space // 2
    edges = jnp.stack([tiles[:, 0], tiles[:, :, width - 1], tiles[:, width - 1], tiles[:, :, 0]], axis=0)
    lines = halo(space, neighbours, rotations, edges)
    count = lax.dynamic_slice_in_dim(tile_counts, lax.axis_index("space"), 1, 0)
    result, grads, small = block(count, tiles, cotan, lines, depth_kernel, depth_bias, norm_gain, norm_bias,
                                 weight_in, bias_in, weight_out, bias_out, layer_scale)
    whole, small = reduce_all(near, far, far // 2, grads, small)
    whole = whole.reshape(2 * chans, hid)
    grad_win = whole[:chans].astype(F32)
    grad_wout = whole[chans:].T.astype(F32)
    return result[None], grad_win, grad_wout, small[14:14 + hid // chans].reshape(hid), small[:14]


def solution(mesh):
    placed = P("dp", "space", None, None, None)
    return jax.shard_map(
        functools.partial(local, shape=dict(mesh.shape)),
        mesh=mesh,
        in_specs=(placed, placed) + (P(),) * 12,
        out_specs=(placed, P(), P(), P(), P()),
        check_vma=False,
    )
```

time: 450 us -> 105 us (0.23)
  waiting for transfers between devices: 249 us -> 0 us
  Pallas kernels: 0 us -> 92.3 us
  blocking collectives: 75.4 us -> 0 us
  matrix products: 45.3 us -> 0 us
  other arithmetic: 35.6 us -> 0.81 us
  local copies, waits for them, and re-layouts: 29.7 us -> 10.7 us
  between operations: 14.4 us -> 0.71 us
    psum x1 -> x0, waiting for transfers between devices: 158 us -> none  [local(): lax.psum((grad_win, grad_wout, grad_bin, channel), ('dp', 'space'))]
    pallas_call x0 -> x3, Pallas kernels: none -> 92.3 us  [the longest x1 47.3 us: reduce_all(): pl.pallas_call(functools.partial(reduce_kernel, near, far, ring), in_spec...]
    all_gather x1 -> x0, waiting for transfers between devices: 90.3 us -> none  [local(): every_border = lax.all_gather(border, 'space', axis=1, tiled=True)]
    psum x1 -> x0, blocking collectives: 75.4 us -> none  [local(): lax.psum((grad_win, grad_wout, grad_bin, channel), ('dp', 'space'))]
    dot_general x6 -> x0, matrix products: 45.3 us -> none  [the longest x1 14.1 us: tile_block(): lax.dot_general(branch, weight_out, contract_cols, preferred_element_type...]
    reduce_sum x5 -> x0, other arithmetic: 26.5 us -> none  [the longest x1 7.93 us: tile_block(): grad_dbias = jnp.sum(dconv, axis=0)]
    gather x2 -> x0, local copies, waits for them, and re-layouts: 8.9 us -> none  [local(): lines = every_border[:, my_nbrs[:, :, None], places[my_turns, sides]]]
    mul x1 -> x0, other arithmetic: 6.83 us -> none  [tile_block(): nhat = centre * inv_std]
  transfers between devices with their start and end apart: 2 -> 0, of which waited for: 2 -> 0; matrix products, arithmetic and copies ran while one was open for 5% -> 0% of each run, Pallas kernels for 0% -> 0%
where the time goes in v1:
time: 105 us
  Pallas kernels  92.3 us (88%)
  local copies, waits for them, and re-layouts  10.7 us (10%)
    pallas_call x1, Pallas kernels, reduce_all(): pl.pallas_call(functools.partial(reduce_kernel, near, far, ring), in_spec...  47.3 us
    pallas_call x1, Pallas kernels, halo(): pl.pallas_call(functools.partial(halo_kernel, space), in_specs=[smem, sme...  25.5 us
    pallas_call x1, Pallas kernels, block(): pl.pallas_call(block_kernel, grid=(slots,), in_specs=[pl.BlockSpec(memory...  19.6 us
    unnamed x10, local copies, waits for them, and re-layouts  4.01 us

profile of v1, /device:TPU:1, one launch (start us, length us, event | category | flops | bytes accessed | tf_op | source)
XLA Modules:
  0.0 104.5 jit_solution(3548094386640023321)
XLA Ops:
  0.6 1.2 %dynamic_slice.3.count = s32[1]{0:T(128)} dynamic-slice(s32[32]{0:T(128)} %param.18, s32[]{:T(128)S(6)} %select_n.3), dynamic_slice_sizes={1} | dynamic-slice | bytes 12 | tf_op jit(solution)/shard_map/dynamic_slice | solution.py:411
  1.9 1.3 %reshape.41.taps_w = f32[9,1,128]{2,1,0:T(1,128)} reshape(f32[3,3,128]{2,1,0:T(4,128)} %param.19) | data formatting | bytes 9216 | tf_op jit(solution)/shard_map/reshape | solution.py:172
  3.2 0.8 copy.27.nbrs
  4.0 0.8 copy.28.turns
  4.7 0.8 slice_bitcast_fusion.1
  5.6 1.3 %fusion = (bf16[4,48,1,128]{3,2,1,0:T(2,128)(2,1)S(1)}, bf16[4,48,1,128]{3,2,1,0:T(2,128)(2,1)S(1)}) fusion(bf16[4,48,48,128]{3,2,1,0:T(8,128)(2,1)} %bitcast.31), kind=kLoop, calls=%fused_computation.8 | loop fusion | bytes 196608 | tf_op jit(solution)/shard_map/slice | solution.py:409
  6.9 25.5 %shard_map.173.lines = bf16[4,4,48,128]{3,2,1,0:T(8,128)(2,1)S(1)} custom-call(s32[128,4]{1,0:T(8,128)S(1)} %copy.27.nbrs, s32[128,4]{1,0:T(8,128)S(1)} %copy.28.turns, bf16[4,4,48,128]{3,2,1,0:T(8,128)(2,1)S(1)} %pad_maximum_fusion.edges), custom_call_target="tpu_custom_call" | custom-call | tf_op jit(solution)/shard_map/pallas_call | solution.py:244
  32.4 0.0 copy-start
  32.4 0.7 copy-done
  33.1 19.6 %shard_map.174 = (bf16[4,48,48,128]{3,2,1,0:T(8,128)(2,1)}, f32[256,512]{1,0:T(8,128)}, f32[24,128]{1,0:T(8,128)}) custom-call(s32[1]{0:T(128)} %dynamic_slice.3.count, bf16[4,48,48,128]{3,2,1,0:T(8,128)(2,1)} %bitcast.32, bf16[4,48,48,128]{3,2,1,0:T(8,128)(2,1)} %bitcast.33, bf16[4,4,48,128]{3,2,1,0:T(8,128)(2,1)} %copy-done, f32[9,1,128]{2,1,0:T(1,128)} %reshape.41.taps_w, ...), custom_call_target="tpu_custom_call" | custom-call | tf_op jit(solution)/shard_map/pallas_call | solution.py:156
  52.7 0.0 copy-start.1
  52.7 1.0 copy-done.1
  53.7 0.0 copy-start.2
  53.7 0.7 copy-done.2
  54.4 47.3 %shard_map.175 = (bf16[16,16,512]{2,1,0:T(8,128)(2,1)S(1)}, f32[24,128]{1,0:T(8,128)S(1)}) custom-call(f32[256,512]{1,0:T(8,128)S(1)} %copy-done.1, f32[24,128]{1,0:T(8,128)S(1)} %copy-done.2), custom_call_target="tpu_custom_call" | custom-call | tf_op jit(solution)/shard_map/pallas_call | solution.py:381
  101.7 0.6 slice_bitcast_fusion.2
  102.3 0.6 slice.33
  102.9 0.8 bitcast_convert_fusion
  103.7 0.8 copy.29
  (4 shorter events, 0.1 us)
Async XLA Ops:
  32.4 0.7 copy-start
  52.7 1.0 copy-start.1
  53.7 0.7 copy-start.2

commit v2 on v0

v2 whole, which is shorter than its diff:
```python
import functools
import math

import jax
import jax.numpy as jnp
from jax import lax
from jax.experimental import pallas as pl
from jax.experimental.pallas import tpu as pltpu
from jax.sharding import PartitionSpec as P

F32, BF16 = jnp.float32, jnp.bfloat16
MESH = pl.DeviceIdType.MESH
PITCH = 64
CONV_ROWS = 8
LAST_ROWS = 8
GROUP = 64
COMM = True


def over_rows(a):
    return jnp.sum(a.reshape(-1, 8, a.shape[-1]), axis=0)


def contract_rows(a, b):
    return lax.dot_general(a, b, (((0,), (0,)), ((), ())), preferred_element_type=F32)


def remote(src, dst, send_sem, recv_sem, device):
    return pltpu.make_async_remote_copy(
        src_ref=src, dst_ref=dst, send_sem=send_sem, recv_sem=recv_sem, device_id=device, device_id_type=MESH
    )


def loop(lo, hi, body, unroll=1):
    def step(i, c):
        body(i)
        return c

    lax.fori_loop(lo, hi, step, 0, unroll=unroll)


def block_kernel(space, near, nbrs, turns, counts, fields, cotangent, taps_w, dbias, gain, nbias, win, bin_, wout,
                 bout, scale, out, grad_win, grad_wout, small_out,
                 tile, cotan, frame, win_t, wout_t, nhat_s, inv_s, normed_s, branch_s, proj_s, dnorm_s, act_s, dpre_s,
                 cot_s, grads, sums, bsum, small, cand, outgo, income, halves, got, mid, far_got, spread, whole,
                 small_got, small_mid, small_far,
                 load_sem, halo_send, halo_recv, near_sem, far_sem, back_sem, sn_sem, sf_sem):
    slots, width, _, chans = tile.shape
    hid = win.shape[1]
    hh = hid // 2
    area = width * width
    main = slots * area
    m = act_s.shape[0]
    picks = 4 * slots
    far = space // 2
    if COMM:
        dp, me = lax.axis_index("dp"), lax.axis_index("space")
        core, plane = lax.rem(me, 2), me // 2
        a = dp * 2 + core
    else:
        me = 0
    loads = []
    for t in range(slots):
        loads.append((pltpu.make_async_copy(fields.at[t], tile.at[t], load_sem.at[0, t]),
                      pltpu.make_async_copy(cotangent.at[t], cotan.at[t], load_sem.at[1, t])))
    for t in range(slots):
        loads[t][0].start()
    for t in range(slots):
        loads[t][1].start()

    def near_id(o):
        p = lax.rem(a + o, near)
        return p, (p // 2, plane * 2 + lax.rem(p, 2))

    def far_id(o):
        p = lax.rem(plane + o, far)
        return p, (dp, p * 2 + core)

    if COMM:
        barrier = pltpu.get_barrier_semaphore()
        loop(1, space, lambda o: pl.semaphore_signal(
            barrier, inc=1, device_id=(dp, lax.rem(me + o, space)), device_id_type=MESH))
        loop(1, near, lambda o: pl.semaphore_signal(barrier, inc=1, device_id=near_id(o)[1], device_id_type=MESH))

    win_t[...] = win[...].T
    for h in range(2):
        wout_t[h] = wout[h * hh:(h + 1) * hh, :].T
    grads[...] = jnp.zeros_like(grads)
    sums[...] = jnp.zeros_like(sums)
    bsum[...] = jnp.zeros_like(bsum)

    def clear(t):
        frame[t, 0:PITCH, :] = jnp.zeros((PITCH, chans), F32)
        frame[t, pl.ds((width + 1) * PITCH, PITCH + 8), :] = jnp.zeros((PITCH + 8, chans), F32)

        def side(r):
            frame[t, pl.ds(pl.multiple_of((r + 1) * PITCH, 8), 8), :] = jnp.zeros((8, chans), F32)
            frame[t, pl.ds(pl.multiple_of((r + 1) * PITCH + 8 + width, 8), 8), :] = jnp.zeros((8, chans), F32)
            frame[t, pl.ds(pl.multiple_of((r + 1) * PITCH + 8, 8), width), :] = tile[t, r].astype(F32)

        loop(0, width, side, 4)

    def edge_of(k, q):
        t = k
        if q == 0:
            return frame[t, pl.ds(PITCH + 8, width), :]
        if q == 1:
            return frame[t, pl.ds(PITCH + 7 + width, width, stride=PITCH), :]
        if q == 2:
            return frame[t, pl.ds(width * PITCH + 8, width), :]
        return frame[t, pl.ds(PITCH + 8, width, stride=PITCH), :]

    def pick_code(nbr, turn, side):
        edge = (turn + (side + 2)) & 3
        flip = ((turn + (side & 1)) >> 1) & 1
        return flip * picks + 4 * (nbr & (slots - 1)) + edge

    for t in range(slots):
        loads[t][0].wait()
    loop(0, slots, clear)
    i = lax.broadcasted_iota(jnp.int32, (width, width), 0)
    j = lax.broadcasted_iota(jnp.int32, (width, width), 1)
    mirror = (i + j == width - 1).astype(BF16)

    def candidates(t):
        for q in range(4):
            line = edge_of(t, q).astype(BF16)
            cand[4 * t + q] = line
            cand[picks + 4 * t + q] = jnp.dot(mirror, line, preferred_element_type=F32).astype(BF16)

    loop(0, slots, candidates)

    if COMM:
        def pick(o):
            peer = lax.rem(me + o, space)
            code = jnp.int32(0)
            for k in range(picks):
                slot, side = peer * slots + k // 4, k % 4
                nbr = nbrs[side, slot]
                code = jnp.where(nbr // slots == me, pick_code(nbr, turns[side, slot], side), code)
            outgo[o] = cand[code]

        loop(0, space, pick)
        income[me] = outgo[0]
        pl.semaphore_wait(barrier, space + near - 2)

        loop(1, space, lambda o: remote(
            outgo.at[o], income.at[me], halo_send.at[o], halo_recv.at[me], (dp, lax.rem(me + o, space))).start())

    for t in range(slots):
        loads[t][1].wait()

    count = counts[me]
    px = lax.broadcasted_iota(jnp.int32, (width, chans), 0)
    inner = ((px > 0) & (px < width - 1)).astype(F32)

    def norm_rows(conv, at):
        x = conv - jnp.mean(conv, axis=-1, keepdims=True)
        iv = lax.rsqrt(jnp.mean(x * x, axis=-1, keepdims=True) + 1e-06)
        nhat = x * iv
        sl = pl.ds(pl.multiple_of(at, 16), width)
        inv_s[sl, :] = jnp.broadcast_to(iv, (width, chans))
        nhat_s[sl, :] = nhat
        normed_s[sl, :] = (nhat * gain[...] + nbias[...]).astype(BF16)

    per = width // CONV_ROWS

    def conv_chunk(step):
        t = step // per
        top = (step - t * per) * CONV_ROWS
        live = jnp.where(t < count, 1.0, 0.0)
        kern = [[taps_w[x, y:y + 1, :] for y in range(3)] for x in range(3)]
        bias = dbias[...]
        conv = {}
        for fr in range(CONV_ROWS + 2):
            base = (top + fr) * PITCH + 7
            win3 = [frame[t, pl.ds(base + b, width), :] for b in range(3)]
            for x in range(3):
                r = fr - x
                if 0 <= r < CONV_ROWS:
                    acc = conv.get(r, bias)
                    for b in range(3):
                        acc = acc + win3[b] * kern[x][b]
                    conv[r] = acc
            r = fr - 2
            if r >= 0:
                at = t * area + (top + r) * width
                norm_rows(conv.pop(r), at)
                inside = jnp.where((top + r > 0) & (top + r < width - 1), live, 0.0)
                g = cotan[t, top + r].astype(F32) * inside
                branch_s[pl.ds(pl.multiple_of(at, 16), width), :] = (g * (scale[...] * inner)).astype(BF16)

    loop(0, slots * per, conv_chunk)

    def border(t):
        live = jnp.where(t < count, 1.0, 0.0)
        kern = [[taps_w[x, y:y + 1, :] for y in range(3)] for x in range(3)]
        for s in range(4):
            if COMM:
                line = income[nbrs[s, me * slots + t] // slots]
            else:
                line = cand[pick_code(nbrs[s, t], turns[s, t], s)]
            line = line.astype(F32)
            if s == 0:
                frame[t, pl.ds(8, width), :] = line
            elif s == 1:
                frame[t, pl.ds(PITCH + 8 + width, width, stride=PITCH), :] = line
            elif s == 2:
                frame[t, pl.ds((width + 1) * PITCH + 8, width), :] = line
            else:
                frame[t, pl.ds(PITCH + 7, width, stride=PITCH), :] = line

        def cots(r):
            cot_s[pl.ds(pl.multiple_of(r * 16, 8), 8), :] = cotan[t, r, 0:16, :].astype(F32)[0:8]
            cot_s[pl.ds(pl.multiple_of(r * 16 + 8, 8), 8), :] = cotan[t, r, width - 16:width, :].astype(F32)[8:16]

        loop(0, width, cots, 4)
        for s in range(4):
            acc = dbias[...]
            for x in range(3):
                for b in range(3):
                    if s == 0:
                        w = frame[t, pl.ds(x * PITCH + 7 + b, width), :]
                    elif s == 1:
                        w = frame[t, pl.ds(x * PITCH + 6 + width + b, width, stride=PITCH), :]
                    elif s == 2:
                        w = frame[t, pl.ds((width - 1 + x) * PITCH + 7 + b, width), :]
                    else:
                        w = frame[t, pl.ds(x * PITCH + 7 + b, width, stride=PITCH), :]
                    acc = acc + w * taps_w[x, b:b + 1, :]
            at = main + (t * 4 + s) * width
            norm_rows(acc, at)
            if s == 0:
                g = cotan[t, 0].astype(F32)
            elif s == 1:
                g = cot_s[pl.ds(15, width, stride=16), :] * inner
            elif s == 2:
                g = cotan[t, width - 1].astype(F32)
            else:
                g = cot_s[pl.ds(0, width, stride=16), :] * inner
            branch_s[pl.ds(pl.multiple_of(at, 16), width), :] = (g * live * scale[...]).astype(BF16)

    def hidden(h, step):
        base = pl.multiple_of(step * m, 16)
        normed = normed_s[pl.ds(base, m), :]
        branch = branch_s[pl.ds(base, m), :]
        hs = pl.ds(h * hh, hh)
        pre_h = jnp.dot(normed, win[:, hs], preferred_element_type=F32)
        dact_h = jnp.dot(branch, wout_t[h], preferred_element_type=F32)
        bs = jnp.zeros((8, hh), F32)
        for q in range(0, m, GROUP):
            pre = pre_h[q:q + GROUP] + bin_[:, hs]
            ph = 0.5 * lax.erf(pre * (1.0 / math.sqrt(2.0))) + 0.5
            act_s[pl.ds(q, GROUP), :] = (pre * ph).astype(BF16)
            slope = ph + pre * (jnp.exp(-0.5 * pre * pre) * (1.0 / math.sqrt(2.0 * math.pi)))
            dpre = dact_h[q:q + GROUP] * slope
            bs = bs + over_rows(dpre)
            dpre_s[pl.ds(q, GROUP), :] = dpre.astype(BF16)
        bsum[h] += bs
        act = act_s[...]
        dpre = dpre_s[...]
        grads[h, 0:chans, :] += contract_rows(normed, dpre)
        grads[h, chans:2 * chans, :] += contract_rows(branch, act)
        proj = jnp.dot(act, wout[hs, :], preferred_element_type=F32)
        dnorm = jnp.dot(dpre, win_t[hs, :], preferred_element_type=F32)
        rows = pl.ds(base, m)
        if h == 0:
            proj_s[rows, :] = proj
            dnorm_s[rows, :] = dnorm
        else:
            proj_s[rows, :] += proj
            dnorm_s[rows, :] += dnorm

    def send_near(h):
        prows = 2 * chans // near
        for p in range(near):
            halves[h, p] = grads[h, p * prows:(p + 1) * prows, :].astype(BF16)
        got[h, a] = halves[h, a]

        def go(o):
            p, device = near_id(o)
            remote(halves.at[h, p], got.at[h, a], near_sem.at[h, 0, o], near_sem.at[h, 1, a], device).start()

        loop(1, near, go)

    def pass_far(h):
        def wait(o):
            p, device = near_id(near - o)
            remote(halves.at[h, p], got.at[h, p], near_sem.at[h, 0, o], near_sem.at[h, 1, p], device).wait()

        loop(1, near, wait)
        tot = got[h, 0].astype(F32)
        for p in range(1, near):
            tot = tot + got[h, p].astype(F32)
        mid[h] = tot.astype(BF16)
        far_got[h, plane] = mid[h]

        def go(o):
            p, device = far_id(o)
            remote(mid.at[h], far_got.at[h, plane], far_sem.at[h, 0, o], far_sem.at[h, 1, plane], device).start()

        loop(1, far, go)

    def pass_back(h):
        def wait(o):
            p, device = far_id(far - o)
            remote(mid.at[h], far_got.at[h, p], far_sem.at[h, 0, o], far_sem.at[h, 1, p], device).wait()

        loop(1, far, wait)
        tot = far_got[h, 0].astype(F32)
        for p in range(1, far):
            tot = tot + far_got[h, p].astype(F32)
        spread[h] = tot.astype(BF16)
        whole[h, a] = spread[h]

        def go(o):
            p, device = near_id(o)
            remote(spread.at[h], whole.at[h, a], back_sem.at[h, 0, o], back_sem.at[h, 1, a], device).start()

        loop(1, near, go)

    def finish(h):
        def wait(o):
            p, device = near_id(near - o)
            remote(spread.at[h], whole.at[h, p], back_sem.at[h, 0, o], back_sem.at[h, 1, p], device).wait()

        loop(1, near, wait)
        prows = 2 * chans // near
        hs = slice(h * hh, (h + 1) * hh)
        full = whole[h].reshape(2 * chans, hh).astype(F32)
        grad_win[:, hs] = full[:chans]
        grad_wout[hs, :] = full[chans:].T

    steps = (main + slots * 4 * width) // m
    loop(0, steps - 1, lambda s: hidden(0, s))
    if COMM:
        def halo_wait(o):
            src = lax.rem(me + space - o, space)
            remote(outgo.at[o], income.at[src], halo_send.at[o], halo_recv.at[src], (dp, src)).wait()

        loop(1, space, halo_wait)
    loop(0, slots, border)
    hidden(0, steps - 1)
    if COMM:
        send_near(0)

    def second(s):
        hidden(1, s)
        if COMM:
            @pl.when(s == 4)
            def _():
                pass_far(0)

            @pl.when(s == 9)
            def _():
                pass_back(0)

    loop(0, steps, second)
    if COMM:
        send_near(1)
        finish(0)

    def merge(t):
        for ref in (proj_s, dnorm_s, nhat_s, inv_s):
            for s in (1, 3, 0, 2):
                v = ref[pl.ds(pl.multiple_of(main + (t * 4 + s) * width, 8), width), :]
                if s == 1:
                    ref[pl.ds(t * area + width - 1, width, stride=width), :] = v
                elif s == 3:
                    ref[pl.ds(t * area, width, stride=width), :] = v
                elif s == 0:
                    ref[pl.ds(pl.multiple_of(t * area, 8), width), :] = v
                else:
                    ref[pl.ds(pl.multiple_of(t * area + area - width, 8), width), :] = v

    loop(0, slots, merge)

    lper = width // LAST_ROWS

    def last(step):
        t = step // lper
        top = (step - t * lper) * LAST_ROWS
        live = jnp.where(t < count, 1.0, 0.0)
        taps = [[jnp.zeros((8, chans), F32)] * 3 for _ in range(3)]
        s_g = s_gp = s_dn = s_dnh = s_dc = jnp.zeros((8, chans), F32)
        dconv = {}
        for fr in range(LAST_ROWS + 2):
            r = fr
            if r < LAST_ROWS:
                sl = pl.ds(pl.multiple_of(t * area + (top + r) * width, 16), width)
                proj = proj_s[sl, :]
                x = tile[t, top + r].astype(F32)
                out[t, top + r] = ((x + scale[...] * (proj + bout[...])) * live).astype(BF16)
                g = cotan[t, top + r].astype(F32)
                s_g = s_g + over_rows(g)
                s_gp = s_gp + over_rows(g * proj)
                dnorm = dnorm_s[sl, :]
                nhat = nhat_s[sl, :]
                dnh = dnorm * nhat
                s_dn = s_dn + over_rows(dnorm)
                s_dnh = s_dnh + over_rows(dnh)
                m1 = jnp.mean(dnorm * gain[...], axis=-1, keepdims=True)
                m2 = jnp.mean(dnh * gain[...], axis=-1, keepdims=True)
                dc = inv_s[sl, :] * (dnorm * gain[...] - m1 - nhat * m2)
                s_dc = s_dc + over_rows(dc)
                dconv[r] = dc
            base = (top + fr) * PITCH + 7
            win3 = [frame[t, pl.ds(base + b, width), :] for b in range(3)]
            for x in range(3):
                r = fr - x
                if 0 <= r < LAST_ROWS:
                    for b in range(3):
                        taps[x][b] = taps[x][b] + over_rows(dconv[r] * win3[b])
            dconv.pop(fr - 2, None)
        for n, s in enumerate([taps[x][b] for x in range(3) for b in range(3)]
                              + [s_dc, s_dnh, s_dn, s_g * live, s_gp * live]):
            sums[n] += s
        if COMM:
            @pl.when(step == slots * lper // 2)
            def _():
                pass_far(1)

    loop(0, slots * lper, last)

    tot = jnp.sum(sums[...], axis=1)
    small[...] = jnp.zeros_like(small)
    small[0:12, :] = tot[0:12]
    small[12:13, :] = tot[12:13] * scale[...]
    small[13:14, :] = tot[13:14] + tot[12:13] * bout[...]
    b = jnp.sum(bsum[...], axis=1)
    per_h = hh // chans
    for h in range(2):
        for n in range(per_h):
            k = 14 + h * per_h + n
            small[k:k + 1, :] = b[h:h + 1, n * chans:(n + 1) * chans]
    if not COMM:
        small_out[...] = small[...]
        for h in range(2):
            grad_win[:, h * hh:(h + 1) * hh] = grads[h, 0:chans, :]
            grad_wout[h * hh:(h + 1) * hh, :] = grads[h, chans:2 * chans, :].T
        return

    small_got[a] = small[...]

    def small_near(o):
        p, device = near_id(o)
        remote(small, small_got.at[a], sn_sem.at[0, o], sn_sem.at[1, a], device).start()

    def small_near_wait(o):
        p, device = near_id(near - o)
        remote(small, small_got.at[p], sn_sem.at[0, o], sn_sem.at[1, p], device).wait()

    def small_far_go(o):
        p, device = far_id(o)
        remote(small_mid, small_far.at[plane], sf_sem.at[0, o], sf_sem.at[1, plane], device).start()

    def small_far_wait(o):
        p, device = far_id(far - o)
        remote(small_mid, small_far.at[p], sf_sem.at[0, o], sf_sem.at[1, p], device).wait()

    loop(1, near, small_near)
    pass_back(1)
    loop(1, near, small_near_wait)
    s = small_got[0]
    for p in range(1, near):
        s = s + small_got[p]
    small_mid[...] = s
    small_far[plane] = s
    loop(1, far, small_far_go)
    finish(1)
    loop(1, far, small_far_wait)
    s = small_far[0]
    for p in range(1, far):
        s = s + small_far[p]
    small_out[...] = s


def block(space, near, nbrs, turns, counts, fields, cotan, kern, dbias, gain, nbias, win, bin_, wout, bout, scale):
    slots, width, _, chans = fields.shape
    hid = win.shape[1]
    hh = hid // 2
    far = space // 2
    main, edge = slots * width * width, slots * 4 * width
    row = lambda v: v.reshape(1, -1)
    smem, vmem, anyw = (pl.BlockSpec(memory_space=s) for s in (pltpu.SMEM, pltpu.VMEM, pl.ANY))
    dma = lambda *s: pltpu.SemaphoreType.DMA(s)
    v = lambda dt, *s: pltpu.VMEM(s, dt)
    piece = (2 * chans // near, hh)
    line = (width, chans)
    return pl.pallas_call(
        functools.partial(block_kernel, space, near),
        in_specs=[smem, smem, smem, anyw, anyw] + [vmem] * 9,
        out_specs=[vmem] * 4,
        out_shape=[jax.ShapeDtypeStruct(fields.shape, BF16), jax.ShapeDtypeStruct((chans, hid), F32),
                   jax.ShapeDtypeStruct((hid, chans), F32), jax.ShapeDtypeStruct((24, chans), F32)],
        scratch_shapes=[
            v(BF16, *fields.shape), v(BF16, *fields.shape), v(F32, slots, (width + 2) * PITCH + 8, chans),
            v(BF16, hid, chans), v(BF16, 2, chans, hh),
            v(F32, main + edge, chans), v(F32, main + edge, chans),
            v(BF16, main + edge, chans), v(BF16, main + edge, chans),
            v(F32, main + edge, chans), v(F32, main + edge, chans),
            v(BF16, edge, hh), v(BF16, edge, hh), v(F32, width * 16, chans),
            v(F32, 2, 2 * chans, hh), v(F32, 14, 8, chans), v(F32, 2, 8, hh), v(F32, 24, chans),
            v(BF16, 8 * slots, *line), v(BF16, space, *line), v(BF16, space, *line),
            v(BF16, 2, near, *piece), v(BF16, 2, near, *piece), v(BF16, 2, *piece), v(BF16, 2, far, *piece),
            v(BF16, 2, *piece), v(BF16, 2, near, *piece),
            v(F32, near, 24, chans), v(F32, 24, chans), v(F32, far, 24, chans),
            dma(2, slots), dma(space), dma(space), dma(2, 2, near), dma(2, 2, far), dma(2, 2, near),
            dma(2, near), dma(2, far)],
        compiler_params=pltpu.CompilerParams(
            vmem_limit_bytes=60 * 2**20, **(dict(collective_id=0, has_side_effects=True) if COMM else {})),
    )(nbrs, turns, counts, fields, cotan, kern, row(dbias), row(gain), row(nbias), win, row(bin_), wout, row(bout),
      row(scale))


def local(fields, cotangent, neighbours, rotations, tile_counts, depth_kernel, depth_bias, norm_gain, norm_bias,
          weight_in, bias_in, weight_out, bias_out, layer_scale, shape):
    chans, hid = weight_in.shape
    result, grad_win, grad_wout, small = block(
        shape["space"], 2 * shape["dp"], neighbours.T, rotations.T, tile_counts, fields[0], cotangent[0], depth_kernel,
        depth_bias, norm_gain, norm_bias, weight_in, bias_in, weight_out, bias_out, layer_scale)
    return result[None], grad_win, grad_wout, small[14:14 + hid // chans].reshape(hid), small[:14]


def solution(mesh):
    placed = P("dp", "space", None, None, None)
    return jax.shard_map(
        functools.partial(local, shape=dict(mesh.shape)),
        mesh=mesh,
        in_specs=(placed, placed) + (P(),) * 12,
        out_specs=(placed, P(), P(), P(), P()),
        check_vma=False,
    )
```

time: 450 us -> 90.3 us (0.20)
  waiting for transfers between devices: 249 us -> 0 us
  Pallas kernels: 0 us -> 81.9 us
  blocking collectives: 75.4 us -> 0 us
  matrix products: 45.3 us -> 0 us
  other arithmetic: 35.6 us -> 0 us
  local copies, waits for them, and re-layouts: 29.7 us -> 7.52 us
  between operations: 14.4 us -> 0.65 us
    psum x1 -> x0, waiting for transfers between devices: 158 us -> none  [local(): lax.psum((grad_win, grad_wout, grad_bin, channel), ('dp', 'space'))]
    all_gather x1 -> x0, waiting for transfers between devices: 90.3 us -> none  [local(): every_border = lax.all_gather(border, 'space', axis=1, tiled=True)]
    pallas_call x0 -> x1, Pallas kernels: none -> 81.9 us  [block(): pl.pallas_call(functools.partial(block_kernel, space, near), in_specs=[sm...]
    psum x1 -> x0, blocking collectives: 75.4 us -> none  [local(): lax.psum((grad_win, grad_wout, grad_bin, channel), ('dp', 'space'))]
    dot_general x6 -> x0, matrix products: 45.3 us -> none  [the longest x1 14.1 us: tile_block(): lax.dot_general(branch, weight_out, contract_cols, preferred_element_type...]
    reduce_sum x5 -> x0, other arithmetic: 26.5 us -> none  [the longest x1 7.93 us: tile_block(): grad_dbias = jnp.sum(dconv, axis=0)]
    gather x2 -> x0, local copies, waits for them, and re-layouts: 8.9 us -> none  [local(): lines = every_border[:, my_nbrs[:, :, None], places[my_turns, sides]]]
    mul x1 -> x0, other arithmetic: 6.83 us -> none  [tile_block(): nhat = centre * inv_std]
  transfers between devices with their start and end apart: 2 -> 0, of which waited for: 2 -> 0; matrix products, arithmetic and copies ran while one was open for 5% -> 0% of each run, Pallas kernels for 0% -> 0%
where the time goes in v2:
time: 90.3 us; the launch traced here: 90.1 us
  Pallas kernels  81.9 us (91%)
  local copies, waits for them, and re-layouts  7.52 us (8%)
    pallas_call x1, Pallas kernels, block(): pl.pallas_call(functools.partial(block_kernel, space, near), in_specs=[sm...  81.9 us
    unnamed x7, local copies, waits for them, and re-layouts  4.94 us

profile of v2, /device:TPU:1, one launch (start us, length us, event | category | flops | bytes accessed | tf_op | source)
XLA Modules:
  0.0 90.1 jit_solution(12167792111154958904)
XLA Ops:
  0.6 81.9 %shard_map.173 = (bf16[4,48,48,128]{3,2,1,0:T(8,128)(2,1)}, f32[128,512]{1,0:T(8,128)}, f32[512,128]{1,0:T(8,128)}, f32[24,128]{1,0:T(8,128)}) custom-call(s32[4,128]{1,0:T(4,128)} %bitcast.16, s32[4,128]{1,0:T(4,128)} %bitcast.17, s32[32]{0:T(128)} %counts.1, bf16[4,48,48,128]{3,2,1,0:T(8,128)(2,1)} %bitcast.13, bf16[4,48,48,128]{3,2,1,0:T(8,128)(2,1)} %bitcast.14, ...), custom_call_target="tpu_custom_call" | custom-call | tf_op jit(solution)/shard_map/pallas_call | solution.py:490
  82.5 1.3 %slice.7 = f32[14,128]{1,0:T(8,128)} slice(f32[24,128]{1,0:T(8,128)} %get-tuple-element.12), slice={[0:14], [0:128]} | slice | bytes 14336 | tf_op jit(solution)/shard_map/slice | solution.py:522
  83.8 1.3 %slice_bitcast_fusion = f32[512]{0:T(512)} fusion(f32[24,128]{1,0:T(8,128)} %get-tuple-element.12), kind=kLoop, calls=%fused_computation | loop fusion | bytes 4096 | tf_op jit(solution)/shard_map/reshape | solution.py:522
  85.1 0.0 copy-start.1
  85.1 0.0 copy-start
  85.1 3.5 %copy.22 = bf16[1,4,48,48,128]{4,3,2,1,0:T(8,128)(2,1)} copy(bf16[1,4,48,48,128]{4,3,2,1,0:T(8,128)(2,1)} %bitcast.15) | data formatting | bytes 4718592
  88.7 0.0 copy-done.1
  88.7 0.7 copy.23
  89.4 0.0 copy-done
  89.4 0.7 copy.24
Async XLA Ops:
  85.1 3.5 %copy-start.1 = (f32[128,512]{1,0:T(8,128)S(1)}, f32[128,512]{1,0:T(8,128)}, u32[]{:S(2)}) copy-start(f32[128,512]{1,0:T(8,128)} %get-tuple-element.19) | copy-start | bytes 786436
  85.1 4.2 %copy-start = (f32[512,128]{1,0:T(8,128)S(1)}, f32[512,128]{1,0:T(8,128)}, u32[]{:S(2)}) copy-start(f32[512,128]{1,0:T(8,128)} %get-tuple-element.20) | copy-start | bytes 786436

commit v3 on v2

--- a/solution.py
+++ b/solution.py
@@ -11,8 +11,8 @@
 F32, BF16 = jnp.float32, jnp.bfloat16
 MESH = pl.DeviceIdType.MESH
 PITCH = 64
-CONV_ROWS = 8
-LAST_ROWS = 8
+CONV_ROWS = 16
+LAST_ROWS = 16
 GROUP = 64
 COMM = True
 
@@ -39,18 +39,32 @@
     lax.fori_loop(lo, hi, step, 0, unroll=unroll)
 
 
-def block_kernel(space, near, nbrs, turns, counts, fields, cotangent, taps_w, dbias, gain, nbias, win, bin_, wout,
-                 bout, scale, out, grad_win, grad_wout, small_out,
-                 tile, cotan, frame, win_t, wout_t, nhat_s, inv_s, normed_s, branch_s, proj_s, dnorm_s, act_s, dpre_s,
-                 cot_s, grads, sums, bsum, small, cand, outgo, income, halves, got, mid, far_got, spread, whole,
+def block_kernel(space, near, fields, cotangent, *refs):
+    slots, width, _, chans = fields.shape
+    held, outs, scratch = refs[:12], refs[12:17], refs[17:]
+    kept, made, rest = scratch[:12], scratch[12:16], scratch[16:]
+    in_sem, out_sem = rest[:2]
+    first = [pltpu.make_async_copy(held[n], kept[n], in_sem.at[n]) for n in range(12)]
+    for n in (9, 11, 0, 1, 2, 3, 4, 5, 6, 7, 8, 10):
+        first[n].start()
+    last = [pltpu.make_async_copy(made[n], outs[n + 1], out_sem.at[n]) for n in range(4)]
+    body(space, near, fields, cotangent, *kept, outs[0], *made, first, last, *rest[2:])
+
+
+def body(space, near, fields, cotangent, nbrs, turns, counts, taps_w, dbias, gain, nbias, bin_, scale, win, bout, wout,
+         out, grad_win, grad_wout, channel_out, bias_out, first, final_copies,
+                 tile, cotan, frame, win_t, wout_t, win_h, nhat_s, inv_s, normed_s, branch_s, act_all, dpre_all,
+                 pre_a, pre_b, dact_a, dact_b, act_a, act_b, dpre_a, dpre_b, proj_b, dnorm_b, rows_a, rows_b, result,
+                 cot_s, codes, grads, sums, bsum, small, cand, outgo, income, halves, got, mid, far_got, spread, whole,
                  small_got, small_mid, small_far,
-                 load_sem, halo_send, halo_recv, near_sem, far_sem, back_sem, sn_sem, sf_sem):
+                 load_sem, out_sem, halo_send, halo_recv, near_sem, far_sem, back_sem, sn_sem, sf_sem):
     slots, width, _, chans = tile.shape
     hid = win.shape[1]
     hh = hid // 2
     area = width * width
     main = slots * area
-    m = act_s.shape[0]
+    m = act_a.shape[0]
+    shift = slots.bit_length() - 1
     picks = 4 * slots
     far = space // 2
     if COMM:
@@ -76,6 +90,8 @@
         p = lax.rem(plane + o, far)
         return p, (dp, p * 2 + core)
 
+    for c in first:
+        c.wait()
     if COMM:
         barrier = pltpu.get_barrier_semaphore()
         loop(1, space, lambda o: pl.semaphore_signal(
@@ -84,10 +100,31 @@
 
     win_t[...] = win[...].T
     for h in range(2):
+        win_h[h] = win[:, h * hh:(h + 1) * hh]
         wout_t[h] = wout[h * hh:(h + 1) * hh, :].T
     grads[...] = jnp.zeros_like(grads)
     sums[...] = jnp.zeros_like(sums)
     bsum[...] = jnp.zeros_like(bsum)
+    act_b[...] = jnp.zeros_like(act_b)
+    dpre_b[...] = jnp.zeros_like(dpre_b)
+
+    def pick_code(k, nbr, turn):
+        side = k & 3
+        edge = (turn + (side + 2)) & 3
+        flip = ((turn + (side & 1)) >> 1) & 1
+        return flip * picks + 4 * (nbr & (slots - 1)) + edge
+
+    if COMM:
+        def scan(o):
+            peer = lax.rem(me + o, space)
+            hit = jnp.int32(0)
+            for k in range(picks):
+                nbr = nbrs[k & 3, peer * slots + (k >> 2)]
+                hit = jnp.where((nbr >> shift) == me, k, hit)
+            slot = peer * slots + (hit >> 2)
+            codes[o] = pick_code(hit, nbrs[hit & 3, slot], turns[hit & 3, slot])
+
+        loop(0, space, scan)
 
     def clear(t):
         frame[t, 0:PITCH, :] = jnp.zeros((PITCH, chans), F32)
@@ -110,14 +147,9 @@
             return frame[t, pl.ds(width * PITCH + 8, width), :]
         return frame[t, pl.ds(PITCH + 8, width, stride=PITCH), :]
 
-    def pick_code(nbr, turn, side):
-        edge = (turn + (side + 2)) & 3
-        flip = ((turn + (side & 1)) >> 1) & 1
-        return flip * picks + 4 * (nbr & (slots - 1)) + edge
-
     for t in range(slots):
         loads[t][0].wait()
-    loop(0, slots, clear)
+        clear(t)
     i = lax.broadcasted_iota(jnp.int32, (width, width), 0)
     j = lax.broadcasted_iota(jnp.int32, (width, width), 1)
     mirror = (i + j == width - 1).astype(BF16)
@@ -131,16 +163,10 @@
     loop(0, slots, candidates)
 
     if COMM:
-        def pick(o):
-            peer = lax.rem(me + o, space)
-            code = jnp.int32(0)
-            for k in range(picks):
-                slot, side = peer * slots + k // 4, k % 4
-                nbr = nbrs[side, slot]
-                code = jnp.where(nbr // slots == me, pick_code(nbr, turns[side, slot], side), code)
-            outgo[o] = cand[code]
-
-        loop(0, space, pick)
+        def gather(o):
+            outgo[o] = cand[codes[o]]
+
+        loop(0, space, gather, 4)
         income[me] = outgo[0]
         pl.semaphore_wait(barrier, space + near - 2)
 
@@ -197,9 +223,9 @@
         kern = [[taps_w[x, y:y + 1, :] for y in range(3)] for x in range(3)]
         for s in range(4):
             if COMM:
-                line = income[nbrs[s, me * slots + t] // slots]
+                line = income[nbrs[s, me * slots + t] >> shift]
             else:
-                line = cand[pick_code(nbrs[s, t], turns[s, t], s)]
+                line = cand[pick_code(s, nbrs[s, t], turns[s, t])]
             line = line.astype(F32)
             if s == 0:
                 frame[t, pl.ds(8, width), :] = line
@@ -240,36 +266,41 @@
                 g = cot_s[pl.ds(0, width, stride=16), :] * inner
             branch_s[pl.ds(pl.multiple_of(at, 16), width), :] = (g * live * scale[...]).astype(BF16)
 
-    def hidden(h, step):
-        base = pl.multiple_of(step * m, 16)
-        normed = normed_s[pl.ds(base, m), :]
-        branch = branch_s[pl.ds(base, m), :]
-        hs = pl.ds(h * hh, hh)
-        pre_h = jnp.dot(normed, win[:, hs], preferred_element_type=F32)
-        dact_h = jnp.dot(branch, wout_t[h], preferred_element_type=F32)
+    steps = (main + slots * 4 * width) // m
+    total = 2 * steps
+
+    def place(k):
+        h = k // steps
+        return h, pl.ds(pl.multiple_of((k - h * steps) * m, 16), m)
+
+    def ahead(k, pre_s, dact_s):
+        h, rows = place(k)
+        pre_s[...] = jnp.dot(normed_s[rows, :], win_h[h], preferred_element_type=F32)
+        dact_s[...] = jnp.dot(branch_s[rows, :], wout_t[h], preferred_element_type=F32)
+
+    def behind(k, act_s, dpre_s):
+        h, rows = place(k)
+        act = act_s[...]
+        dpre = dpre_s[...]
+        act_all[h, rows, :] = act
+        dpre_all[h, rows, :] = dpre
+        grads[h, 0:chans, :] += contract_rows(normed_s[rows, :], dpre)
+        grads[h, chans:2 * chans, :] += contract_rows(branch_s[rows, :], act)
+
+    def hidden(k, pre_s, dact_s, act_s, dpre_s):
+        h, _ = place(k)
+        bias = bin_[h]
         bs = jnp.zeros((8, hh), F32)
         for q in range(0, m, GROUP):
-            pre = pre_h[q:q + GROUP] + bin_[:, hs]
+            sl = pl.ds(q, GROUP)
+            pre = pre_s[sl, :] + bias
             ph = 0.5 * lax.erf(pre * (1.0 / math.sqrt(2.0))) + 0.5
-            act_s[pl.ds(q, GROUP), :] = (pre * ph).astype(BF16)
+            act_s[sl, :] = (pre * ph).astype(BF16)
             slope = ph + pre * (jnp.exp(-0.5 * pre * pre) * (1.0 / math.sqrt(2.0 * math.pi)))
-            dpre = dact_h[q:q + GROUP] * slope
+            dpre = dact_s[sl, :] * slope
             bs = bs + over_rows(dpre)
-            dpre_s[pl.ds(q, GROUP), :] = dpre.astype(BF16)
+            dpre_s[sl, :] = dpre.astype(BF16)
         bsum[h] += bs
-        act = act_s[...]
-        dpre = dpre_s[...]
-        grads[h, 0:chans, :] += contract_rows(normed, dpre)
-        grads[h, chans:2 * chans, :] += contract_rows(branch, act)
-        proj = jnp.dot(act, wout[hs, :], preferred_element_type=F32)
-        dnorm = jnp.dot(dpre, win_t[hs, :], preferred_element_type=F32)
-        rows = pl.ds(base, m)
-        if h == 0:
-            proj_s[rows, :] = proj
-            dnorm_s[rows, :] = dnorm
-        else:
-            proj_s[rows, :] += proj
-            dnorm_s[rows, :] += dnorm
 
     def send_near(h):
         prows = 2 * chans // near
@@ -331,37 +362,43 @@
         grad_win[:, hs] = full[:chans]
         grad_wout[hs, :] = full[chans:].T
 
-    steps = (main + slots * 4 * width) // m
-    loop(0, steps - 1, lambda s: hidden(0, s))
+    def halo_wait(o):
+        src = lax.rem(me + space - o, space)
+        remote(outgo.at[o], income.at[src], halo_send.at[o], halo_recv.at[src], (dp, src)).wait()
+
+    def stage(j):
+        k = 2 * j
+
+        @pl.when(j == (steps - 2) // 2)
+        def _():
+            if COMM:
+                loop(1, space, halo_wait)
+            loop(0, slots, border)
+
+        if COMM:
+            @pl.when(j == (steps + 2) // 2)
+            def _():
+                send_near(0)
+
+        behind(jnp.maximum(k - 1, 0), act_b, dpre_b)
+        ahead(k + 1, pre_b, dact_b)
+        hidden(k, pre_a, dact_a, act_a, dpre_a)
+        behind(k, act_a, dpre_a)
+        ahead(jnp.minimum(k + 2, total - 1), pre_a, dact_a)
+        hidden(k + 1, pre_b, dact_b, act_b, dpre_b)
+
+    ahead(0, pre_a, dact_a)
+    loop(0, steps, stage)
+    behind(total - 1, act_b, dpre_b)
     if COMM:
-        def halo_wait(o):
-            src = lax.rem(me + space - o, space)
-            remote(outgo.at[o], income.at[src], halo_send.at[o], halo_recv.at[src], (dp, src)).wait()
-
-        loop(1, space, halo_wait)
-    loop(0, slots, border)
-    hidden(0, steps - 1)
-    if COMM:
-        send_near(0)
-
-    def second(s):
-        hidden(1, s)
-        if COMM:
-            @pl.when(s == 4)
-            def _():
-                pass_far(0)
-
-            @pl.when(s == 9)
-            def _():
-                pass_back(0)
-
-    loop(0, steps, second)
-    if COMM:
+        pass_far(0)
         send_near(1)
-        finish(0)
+    edge_rows = pl.ds(main, m)
+    dnorm_b[...] = jnp.dot(jnp.concatenate([dpre_all[0, edge_rows, :], dpre_all[1, edge_rows, :]], axis=1), win_t[...],
+                           preferred_element_type=F32)
 
     def merge(t):
-        for ref in (proj_s, dnorm_s, nhat_s, inv_s):
+        for ref in (nhat_s, inv_s):
             for s in (1, 3, 0, 2):
                 v = ref[pl.ds(pl.multiple_of(main + (t * 4 + s) * width, 8), width), :]
                 if s == 1:
@@ -376,25 +413,54 @@
     loop(0, slots, merge)
 
     lper = width // LAST_ROWS
-
-    def last(step):
+    lrows = LAST_ROWS * width
+
+    def product(step, both, weight, rows_s):
+        rows = pl.ds(pl.multiple_of(step * lrows, 16), lrows)
+        rows_s[...] = jnp.dot(jnp.concatenate([both[0, rows, :], both[1, rows, :]], axis=1), weight[...],
+                              preferred_element_type=F32)
+
+    def piped(lo, hi, both, weight, use):
+        product(lo, both, weight, rows_a)
+
+        def pair(j):
+            k = lo + 2 * j
+            product(k + 1, both, weight, rows_b)
+            use(k, rows_a)
+            product(jnp.minimum(k + 2, hi - 1), both, weight, rows_a)
+            use(k + 1, rows_b)
+
+        loop(0, (hi - lo) // 2, pair)
+
+    def with_border(t, top, rows_s, edges):
+        at = t * 4 * width
+        rows_s[pl.ds(width - 1, LAST_ROWS, stride=width), :] = edges[pl.ds(pl.multiple_of(at + width + top, 8), LAST_ROWS), :]
+        rows_s[pl.ds(0, LAST_ROWS, stride=width), :] = edges[pl.ds(pl.multiple_of(at + 3 * width + top, 8), LAST_ROWS), :]
+        out = []
+        for r in range(LAST_ROWS):
+            v = rows_s[pl.ds(r * width, width), :]
+            if r == 0:
+                v = jnp.where(top == 0, edges[pl.ds(pl.multiple_of(at, 8), width), :], v)
+            if r == LAST_ROWS - 1:
+                v = jnp.where(top == width - LAST_ROWS, edges[pl.ds(pl.multiple_of(at + 2 * width, 8), width), :], v)
+            out.append(v)
+        return out
+
+    def last(step, rows_s):
         t = step // lper
-        top = (step - t * lper) * LAST_ROWS
+        top = pl.multiple_of((step - t * lper) * LAST_ROWS, 8)
         live = jnp.where(t < count, 1.0, 0.0)
+        start = pl.multiple_of(t * area + top * width, 16)
+        dn = with_border(t, top, rows_s, dnorm_b)
         taps = [[jnp.zeros((8, chans), F32)] * 3 for _ in range(3)]
-        s_g = s_gp = s_dn = s_dnh = s_dc = jnp.zeros((8, chans), F32)
+        s_g = s_dn = s_dnh = s_dc = jnp.zeros((8, chans), F32)
         dconv = {}
         for fr in range(LAST_ROWS + 2):
             r = fr
             if r < LAST_ROWS:
-                sl = pl.ds(pl.multiple_of(t * area + (top + r) * width, 16), width)
-                proj = proj_s[sl, :]
-                x = tile[t, top + r].astype(F32)
-                out[t, top + r] = ((x + scale[...] * (proj + bout[...])) * live).astype(BF16)
-                g = cotan[t, top + r].astype(F32)
-                s_g = s_g + over_rows(g)
-                s_gp = s_gp + over_rows(g * proj)
-                dnorm = dnorm_s[sl, :]
+                sl = pl.ds(pl.multiple_of(start + r * width, 16), width)
+                s_g = s_g + over_rows(cotan[t, top + r].astype(F32))
+                dnorm = dn[r]
                 nhat = nhat_s[sl, :]
                 dnh = dnorm * nhat
                 s_dn = s_dn + over_rows(dnorm)
@@ -412,32 +478,65 @@
                     for b in range(3):
                         taps[x][b] = taps[x][b] + over_rows(dconv[r] * win3[b])
             dconv.pop(fr - 2, None)
-        for n, s in enumerate([taps[x][b] for x in range(3) for b in range(3)]
-                              + [s_dc, s_dnh, s_dn, s_g * live, s_gp * live]):
+        for n, s in enumerate([taps[x][b] for x in range(3) for b in range(3)] + [s_dc, s_dnh, s_dn, s_g * live]):
             sums[n] += s
         if COMM:
-            @pl.when(step == slots * lper // 2)
+            @pl.when(step == slots * lper * 3 // 4)
             def _():
                 pass_far(1)
 
-    loop(0, slots * lper, last)
+    def finalize(step, rows_s):
+        t = step // lper
+        top = pl.multiple_of((step - t * lper) * LAST_ROWS, 8)
+        live = jnp.where(t < count, 1.0, 0.0)
+        start = pl.multiple_of(t * area + top * width, 16)
+        proj = with_border(t, top, rows_s, proj_b)
+        for r in range(LAST_ROWS):
+            x = tile[t, top + r].astype(F32)
+            result[t, top + r] = ((x + scale[...] * (proj[r] + bout[...])) * live).astype(BF16)
+
+        @pl.when(top == width - LAST_ROWS)
+        def _():
+            pltpu.make_async_copy(result.at[t], out.at[t], out_sem.at[t]).start()
+
+    def finalize_all(lo, hi):
+        piped(lo, hi, act_all, wout, finalize)
+
+    piped(0, slots * lper, dpre_all, win_t, last)
 
     tot = jnp.sum(sums[...], axis=1)
     small[...] = jnp.zeros_like(small)
+    g_proj = jnp.zeros((8, chans), F32)
+    for h in range(2):
+        g_proj = g_proj + over_rows(grads[h, chans:2 * chans, :].T * wout[h * hh:(h + 1) * hh, :].astype(F32))
     small[0:12, :] = tot[0:12]
     small[12:13, :] = tot[12:13] * scale[...]
-    small[13:14, :] = tot[13:14] + tot[12:13] * bout[...]
+    small[13:14, :] = jnp.sum(g_proj, axis=0, keepdims=True) / scale[...] + tot[12:13] * bout[...]
     b = jnp.sum(bsum[...], axis=1)
     per_h = hh // chans
     for h in range(2):
         for n in range(per_h):
             k = 14 + h * per_h + n
             small[k:k + 1, :] = b[h:h + 1, n * chans:(n + 1) * chans]
+    def write_small(v):
+        channel_out[...] = v[0:14]
+        for n in range(hid // chans):
+            bias_out[:, n * chans:(n + 1) * chans] = v[14 + n:15 + n]
+
+    proj_b[...] = jnp.dot(jnp.concatenate([act_all[0, edge_rows, :], act_all[1, edge_rows, :]], axis=1), wout[...],
+                          preferred_element_type=F32)
     if not COMM:
-        small_out[...] = small[...]
+        write_small(small[...])
         for h in range(2):
             grad_win[:, h * hh:(h + 1) * hh] = grads[h, 0:chans, :]
             grad_wout[h * hh:(h + 1) * hh, :] = grads[h, chans:2 * chans, :].T
+        finalize_all(0, slots * lper)
+        for c in final_copies:
+            c.start()
+        for t in range(slots):
+            pltpu.make_async_copy(result.at[t], out.at[t], out_sem.at[t]).wait()
+        for c in final_copies:
+            c.wait()
         return
 
     small_got[a] = small[...]
@@ -459,7 +558,8 @@
         remote(small_mid, small_far.at[p], sf_sem.at[0, o], sf_sem.at[1, p], device).wait()
 
     loop(1, near, small_near)
-    pass_back(1)
+    pass_back(0)
+    finalize_all(0, slots * lper // 2)
     loop(1, near, small_near_wait)
     s = small_got[0]
     for p in range(1, near):
@@ -467,12 +567,49 @@
     small_mid[...] = s
     small_far[plane] = s
     loop(1, far, small_far_go)
+    pass_back(1)
+    finalize_all(slots * lper // 2, slots * lper)
+    finish(0)
+    for t in range(slots):
+        pltpu.make_async_copy(result.at[t], out.at[t], out_sem.at[t]).wait()
     finish(1)
+    for c in final_copies[:2]:
+        c.start()
     loop(1, far, small_far_wait)
     s = small_far[0]
     for p in range(1, far):
         s = s + small_far[p]
-    small_out[...] = s
+    write_small(s)
+    for c in final_copies[2:]:
+        c.start()
+    for c in final_copies:
+        c.wait()
+
+
+def publish_kernel(*refs):
+    n = len(refs) // 2
+    srcs, dsts, sems = refs[:n], refs[n:2 * n], refs[2 * n]
+    copies = []
+    for t in range(srcs[0].shape[0]):
+        copies.append(pltpu.make_async_copy(srcs[0].at[t], dsts[0].at[t], sems.at[len(copies)]))
+    for src, dst in zip(srcs[1:], dsts[1:]):
+        copies.append(pltpu.make_async_copy(src, dst, sems.at[len(copies)]))
+    for c in copies:
+        c.start()
+    for c in copies:
+        c.wait()
+
+
+def publish(*arrays):
+    anyw = pl.BlockSpec(memory_space=pl.ANY)
+    return pl.pallas_call(
+        publish_kernel,
+        in_specs=[anyw] * len(arrays),
+        out_specs=[anyw] * len(arrays),
+        out_shape=[jax.ShapeDtypeStruct(v.shape, v.dtype) for v in arrays],
+        scratch_shapes=[pltpu.SemaphoreType.DMA((arrays[0].shape[0] + len(arrays) - 1,))],
+        compiler_params=pltpu.CompilerParams(vmem_limit_bytes=60 * 2**20),
+    )(*arrays)
 
 
 def block(space, near, nbrs, turns, counts, fields, cotan, kern, dbias, gain, nbias, win, bin_, wout, bout, scale):
@@ -482,44 +619,53 @@
     far = space // 2
     main, edge = slots * width * width, slots * 4 * width
     row = lambda v: v.reshape(1, -1)
-    smem, vmem, anyw = (pl.BlockSpec(memory_space=s) for s in (pltpu.SMEM, pltpu.VMEM, pl.ANY))
+    anyw = pl.BlockSpec(memory_space=pl.ANY)
+    ints = lambda *s: pltpu.SMEM(s, jnp.int32)
     dma = lambda *s: pltpu.SemaphoreType.DMA(s)
     v = lambda dt, *s: pltpu.VMEM(s, dt)
     piece = (2 * chans // near, hh)
     line = (width, chans)
     return pl.pallas_call(
         functools.partial(block_kernel, space, near),
-        in_specs=[smem, smem, smem, anyw, anyw] + [vmem] * 9,
-        out_specs=[vmem] * 4,
+        in_specs=[anyw] * 14,
+        out_specs=[anyw] * 5,
         out_shape=[jax.ShapeDtypeStruct(fields.shape, BF16), jax.ShapeDtypeStruct((chans, hid), F32),
-                   jax.ShapeDtypeStruct((hid, chans), F32), jax.ShapeDtypeStruct((24, chans), F32)],
+                   jax.ShapeDtypeStruct((hid, chans), F32), jax.ShapeDtypeStruct((14, chans), F32),
+                   jax.ShapeDtypeStruct((1, hid), F32)],
         scratch_shapes=[
+            ints(*nbrs.shape), ints(*turns.shape), ints(*counts.shape), v(F32, 3, 3, chans), v(F32, 1, chans),
+            v(F32, 1, chans), v(F32, 1, chans), v(F32, 2, 1, hh), v(F32, 1, chans), v(BF16, chans, hid),
+            v(F32, 1, chans), v(BF16, hid, chans),
+            v(F32, chans, hid), v(F32, hid, chans), v(F32, 14, chans), v(F32, 1, hid), dma(12), dma(4),
             v(BF16, *fields.shape), v(BF16, *fields.shape), v(F32, slots, (width + 2) * PITCH + 8, chans),
-            v(BF16, hid, chans), v(BF16, 2, chans, hh),
+            v(BF16, hid, chans), v(BF16, 2, chans, hh), v(BF16, 2, chans, hh),
             v(F32, main + edge, chans), v(F32, main + edge, chans),
             v(BF16, main + edge, chans), v(BF16, main + edge, chans),
-            v(F32, main + edge, chans), v(F32, main + edge, chans),
-            v(BF16, edge, hh), v(BF16, edge, hh), v(F32, width * 16, chans),
-            v(F32, 2, 2 * chans, hh), v(F32, 14, 8, chans), v(F32, 2, 8, hh), v(F32, 24, chans),
+            v(BF16, 2, main + edge, hh), v(BF16, 2, main + edge, hh),
+            v(F32, edge, hh), v(F32, edge, hh), v(F32, edge, hh), v(F32, edge, hh),
+            v(BF16, edge, hh), v(BF16, edge, hh), v(BF16, edge, hh), v(BF16, edge, hh),
+            v(F32, edge, chans), v(F32, edge, chans), v(F32, LAST_ROWS * width, chans), v(F32, LAST_ROWS * width, chans),
+            v(BF16, *fields.shape),
+            v(F32, width * 16, chans), pltpu.SMEM((space,), jnp.int32),
+            v(F32, 2, 2 * chans, hh), v(F32, 13, 8, chans), v(F32, 2, 8, hh), v(F32, 24, chans),
             v(BF16, 8 * slots, *line), v(BF16, space, *line), v(BF16, space, *line),
             v(BF16, 2, near, *piece), v(BF16, 2, near, *piece), v(BF16, 2, *piece), v(BF16, 2, far, *piece),
             v(BF16, 2, *piece), v(BF16, 2, near, *piece),
             v(F32, near, 24, chans), v(F32, 24, chans), v(F32, far, 24, chans),
-            dma(2, slots), dma(space), dma(space), dma(2, 2, near), dma(2, 2, far), dma(2, 2, near),
+            dma(2, slots), dma(slots), dma(space), dma(space), dma(2, 2, near), dma(2, 2, far), dma(2, 2, near),
             dma(2, near), dma(2, far)],
         compiler_params=pltpu.CompilerParams(
             vmem_limit_bytes=60 * 2**20, **(dict(collective_id=0, has_side_effects=True) if COMM else {})),
-    )(nbrs, turns, counts, fields, cotan, kern, row(dbias), row(gain), row(nbias), win, row(bin_), wout, row(bout),
-      row(scale))
+    )(fields, cotan, nbrs, turns, counts, kern, row(dbias), row(gain), row(nbias), bin_.reshape(2, 1, hh), row(scale),
+      win, row(bout), wout)
 
 
 def local(fields, cotangent, neighbours, rotations, tile_counts, depth_kernel, depth_bias, norm_gain, norm_bias,
           weight_in, bias_in, weight_out, bias_out, layer_scale, shape):
-    chans, hid = weight_in.shape
-    result, grad_win, grad_wout, small = block(
+    result, grad_win, grad_wout, channel, bias = publish(*block(
         shape["space"], 2 * shape["dp"], neighbours.T, rotations.T, tile_counts, fields[0], cotangent[0], depth_kernel,
-        depth_bias, norm_gain, norm_bias, weight_in, bias_in, weight_out, bias_out, layer_scale)
-    return result[None], grad_win, grad_wout, small[14:14 + hid // chans].reshape(hid), small[:14]
+        depth_bias, norm_gain, norm_bias, weight_in, bias_in, weight_out, bias_out, layer_scale))
+    return result[None], grad_win, grad_wout, bias.reshape(-1), channel
 
 
 def solution(mesh):

time: 90.3 us -> 160 us (1.77)
  Pallas kernels: 81.9 us -> 159 us
  local copies, waits for them, and re-layouts: 7.52 us -> 0 us
    pallas_call x1 -> x2, Pallas kernels: 81.9 us -> 159 us  [the longest x1 88.8 us: publish(): pl.pallas_call(publish_kernel, in_specs=[anyw] * len(arrays), out_specs=[...]
    unnamed x7 -> x0, local copies, waits for them, and re-layouts: 4.94 us -> none
where the time goes in v3:
time: 160 us
  Pallas kernels  159 us (99%)
    pallas_call x1, Pallas kernels, publish(): pl.pallas_call(publish_kernel, in_specs=[anyw] * len(arrays), out_specs=[...  88.8 us
    pallas_call x1, Pallas kernels, block(): pl.pallas_call(functools.partial(block_kernel, space, near), in_specs=[an...  70.1 us

profile of v3, /device:TPU:1, one launch (start us, length us, event | category | flops | bytes accessed | tf_op | source)
XLA Modules:
  0.0 159.5 jit_solution(6581621471260383976)
XLA Ops:
  0.6 70.1 %shard_map.173 = (bf16[4,48,48,128]{3,2,1,0:T(8,128)(2,1)}, f32[128,512]{1,0:T(8,128)}, f32[512,128]{1,0:T(8,128)}, f32[14,128]{1,0:T(8,128)}, f32[1,512]{1,0:T(1,128)}) custom-call(bf16[4,48,48,128]{3,2,1,0:T(8,128)(2,1)} %bitcast.12, bf16[4,48,48,128]{3,2,1,0:T(8,128)(2,1)} %bitcast.13, s32[4,128]{1,0:T(4,128)} %bitcast.14, s32[4,128]{1,0:T(4,128)} %bitcast.15, ...), custom_call_target="tpu_custom_call" | custom-call | tf_op jit(solution)/shard_map/pallas_call | solution.py:628
  70.7 88.8 %shard_map.174 = (bf16[4,48,48,128]{3,2,1,0:T(8,128)(2,1)}, f32[128,512]{1,0:T(8,128)}, f32[512,128]{1,0:T(8,128)}, f32[14,128]{1,0:T(8,128)}, f32[1,512]{1,0:T(1,128)}) custom-call(bf16[4,48,48,128]{3,2,1,0:T(8,128)(2,1)} %get-tuple-element.15.refs_0_, f32[128,512]{1,0:T(8,128)} %get-tuple-element.16.refs_1_, f32[512,128]{1,0:T(8,128)} %get-tuple-element.17.refs_2_, ...), custom_call_target="tpu_custom_call" | custom-call | tf_op jit(solution)/shard_map/pallas_call | solution.py:605

commit v4 on v3

--- a/solution.py
+++ b/solution.py
@@ -14,6 +14,7 @@
 CONV_ROWS = 16
 LAST_ROWS = 16
 GROUP = 64
+UNROLL = 2
 COMM = True
 
 
@@ -54,9 +55,9 @@
 def body(space, near, fields, cotangent, nbrs, turns, counts, taps_w, dbias, gain, nbias, bin_, scale, win, bout, wout,
          out, grad_win, grad_wout, channel_out, bias_out, first, final_copies,
                  tile, cotan, frame, win_t, wout_t, win_h, nhat_s, inv_s, normed_s, branch_s, act_all, dpre_all,
-                 pre_a, pre_b, dact_a, dact_b, act_a, act_b, dpre_a, dpre_b, proj_b, dnorm_b, rows_a, rows_b, result,
+                 pre_a, pre_b, dact_a, dact_b, act_a, act_b, dpre_a, dpre_b, proj_b, dnorm_b, rows_a, rows_b,
                  cot_s, codes, grads, sums, bsum, small, cand, outgo, income, halves, got, mid, far_got, spread, whole,
-                 small_got, small_mid, small_far,
+                 small_got, small_mid, small_far, parts,
                  load_sem, out_sem, halo_send, halo_recv, near_sem, far_sem, back_sem, sn_sem, sf_sem):
     slots, width, _, chans = tile.shape
     hid = win.shape[1]
@@ -90,14 +91,14 @@
         p = lax.rem(plane + o, far)
         return p, (dp, p * 2 + core)
 
-    for c in first:
-        c.wait()
     if COMM:
         barrier = pltpu.get_barrier_semaphore()
         loop(1, space, lambda o: pl.semaphore_signal(
             barrier, inc=1, device_id=(dp, lax.rem(me + o, space)), device_id_type=MESH))
         loop(1, near, lambda o: pl.semaphore_signal(barrier, inc=1, device_id=near_id(o)[1], device_id_type=MESH))
 
+    for c in first:
+        c.wait()
     win_t[...] = win[...].T
     for h in range(2):
         win_h[h] = win[:, h * hh:(h + 1) * hh]
@@ -366,20 +367,7 @@
         src = lax.rem(me + space - o, space)
         remote(outgo.at[o], income.at[src], halo_send.at[o], halo_recv.at[src], (dp, src)).wait()
 
-    def stage(j):
-        k = 2 * j
-
-        @pl.when(j == (steps - 2) // 2)
-        def _():
-            if COMM:
-                loop(1, space, halo_wait)
-            loop(0, slots, border)
-
-        if COMM:
-            @pl.when(j == (steps + 2) // 2)
-            def _():
-                send_near(0)
-
+    def pair(k):
         behind(jnp.maximum(k - 1, 0), act_b, dpre_b)
         ahead(k + 1, pre_b, dact_b)
         hidden(k, pre_a, dact_a, act_a, dpre_a)
@@ -387,13 +375,40 @@
         ahead(jnp.minimum(k + 2, total - 1), pre_a, dact_a)
         hidden(k + 1, pre_b, dact_b, act_b, dpre_b)
 
+    def stage(i):
+        @pl.when(i == (steps - 3) // 4)
+        def _():
+            if COMM:
+                loop(1, space, halo_wait)
+            loop(0, slots, border)
+
+        if COMM:
+            @pl.when(i == (steps - 3) // 4 + 1)
+            def _():
+                send_near(0)
+
+        for n in range(UNROLL):
+            pair(2 + 2 * UNROLL * i + 2 * n)
+
     ahead(0, pre_a, dact_a)
-    loop(0, steps, stage)
+    pair(0)
+    loop(0, (steps - 1) // UNROLL, stage)
     behind(total - 1, act_b, dpre_b)
     if COMM:
         pass_far(0)
         send_near(1)
     edge_rows = pl.ds(main, m)
+    g_proj = jnp.zeros((8, chans), F32)
+    for h in range(2):
+        g_proj = g_proj + over_rows(grads[h, chans:2 * chans, :].T * wout[h * hh:(h + 1) * hh, :].astype(F32))
+    parts[...] = jnp.zeros_like(parts)
+    parts[13:14, :] = jnp.sum(g_proj, axis=0, keepdims=True) / scale[...]
+    b = jnp.sum(bsum[...], axis=1)
+    per_h = hh // chans
+    for h in range(2):
+        for n in range(per_h):
+            k = 14 + h * per_h + n
+            parts[k:k + 1, :] = b[h:h + 1, n * chans:(n + 1) * chans]
     dnorm_b[...] = jnp.dot(jnp.concatenate([dpre_all[0, edge_rows, :], dpre_all[1, edge_rows, :]], axis=1), win_t[...],
                            preferred_element_type=F32)
 
@@ -420,11 +435,13 @@
         rows_s[...] = jnp.dot(jnp.concatenate([both[0, rows, :], both[1, rows, :]], axis=1), weight[...],
                               preferred_element_type=F32)
 
-    def piped(lo, hi, both, weight, use):
+    def piped(lo, hi, both, weight, use, hook=None):
         product(lo, both, weight, rows_a)
 
         def pair(j):
             k = lo + 2 * j
+            if hook is not None:
+                hook(j)
             product(k + 1, both, weight, rows_b)
             use(k, rows_a)
             product(jnp.minimum(k + 2, hi - 1), both, weight, rows_a)
@@ -480,11 +497,6 @@
             dconv.pop(fr - 2, None)
         for n, s in enumerate([taps[x][b] for x in range(3) for b in range(3)] + [s_dc, s_dnh, s_dn, s_g * live]):
             sums[n] += s
-        if COMM:
-            @pl.when(step == slots * lper * 3 // 4)
-            def _():
-                pass_far(1)
-
     def finalize(step, rows_s):
         t = step // lper
         top = pl.multiple_of((step - t * lper) * LAST_ROWS, 8)
@@ -493,31 +505,36 @@
         proj = with_border(t, top, rows_s, proj_b)
         for r in range(LAST_ROWS):
             x = tile[t, top + r].astype(F32)
-            result[t, top + r] = ((x + scale[...] * (proj[r] + bout[...])) * live).astype(BF16)
+            tile[t, top + r] = ((x + scale[...] * (proj[r] + bout[...])) * live).astype(BF16)
 
         @pl.when(top == width - LAST_ROWS)
         def _():
-            pltpu.make_async_copy(result.at[t], out.at[t], out_sem.at[t]).start()
+            pltpu.make_async_copy(tile.at[t], out.at[t], out_sem.at[t]).start()
+
+    def small_near(o):
+        p, device = near_id(o)
+        remote(small, small_got.at[a], sn_sem.at[0, o], sn_sem.at[1, a], device).start()
 
     def finalize_all(lo, hi):
         piped(lo, hi, act_all, wout, finalize)
 
-    piped(0, slots * lper, dpre_all, win_t, last)
+    def between(j):
+        if COMM:
+            @pl.when(j == slots * lper // 2 * 2 // 3)
+            def _():
+                pass_far(1)
+
+    piped(0, slots * lper, dpre_all, win_t, last, between)
 
     tot = jnp.sum(sums[...], axis=1)
-    small[...] = jnp.zeros_like(small)
-    g_proj = jnp.zeros((8, chans), F32)
-    for h in range(2):
-        g_proj = g_proj + over_rows(grads[h, chans:2 * chans, :].T * wout[h * hh:(h + 1) * hh, :].astype(F32))
-    small[0:12, :] = tot[0:12]
-    small[12:13, :] = tot[12:13] * scale[...]
-    small[13:14, :] = jnp.sum(g_proj, axis=0, keepdims=True) / scale[...] + tot[12:13] * bout[...]
-    b = jnp.sum(bsum[...], axis=1)
-    per_h = hh // chans
-    for h in range(2):
-        for n in range(per_h):
-            k = 14 + h * per_h + n
-            small[k:k + 1, :] = b[h:h + 1, n * chans:(n + 1) * chans]
+    parts[0:12, :] = tot[0:12]
+    parts[12:13, :] = tot[12:13] * scale[...]
+    parts[13:14, :] += tot[12:13] * bout[...]
+    small[...] = parts[...].astype(BF16)
+    if COMM:
+        small_got[a] = small[...]
+        loop(1, near, small_near)
+
     def write_small(v):
         channel_out[...] = v[0:14]
         for n in range(hid // chans):
@@ -526,7 +543,7 @@
     proj_b[...] = jnp.dot(jnp.concatenate([act_all[0, edge_rows, :], act_all[1, edge_rows, :]], axis=1), wout[...],
                           preferred_element_type=F32)
     if not COMM:
-        write_small(small[...])
+        write_small(parts[...])
         for h in range(2):
             grad_win[:, h * hh:(h + 1) * hh] = grads[h, 0:chans, :]
             grad_wout[h * hh:(h + 1) * hh, :] = grads[h, chans:2 * chans, :].T
@@ -534,17 +551,11 @@
         for c in final_copies:
             c.start()
         for t in range(slots):
-            pltpu.make_async_copy(result.at[t], out.at[t], out_sem.at[t]).wait()
+            pltpu.make_async_copy(tile.at[t], out.at[t], out_sem.at[t]).wait()
         for c in final_copies:
             c.wait()
         return
 
-    small_got[a] = small[...]
-
-    def small_near(o):
-        p, device = near_id(o)
-        remote(small, small_got.at[a], sn_sem.at[0, o], sn_sem.at[1, a], device).start()
-
     def small_near_wait(o):
         p, device = near_id(near - o)
         remote(small, small_got.at[p], sn_sem.at[0, o], sn_sem.at[1, p], device).wait()
@@ -557,28 +568,27 @@
         p, device = far_id(far - o)
         remote(small_mid, small_far.at[p], sf_sem.at[0, o], sf_sem.at[1, p], device).wait()
 
-    loop(1, near, small_near)
     pass_back(0)
     finalize_all(0, slots * lper // 2)
     loop(1, near, small_near_wait)
-    s = small_got[0]
+    s = small_got[0].astype(F32)
     for p in range(1, near):
-        s = s + small_got[p]
-    small_mid[...] = s
-    small_far[plane] = s
+        s = s + small_got[p].astype(F32)
+    small_mid[...] = s.astype(BF16)
+    small_far[plane] = small_mid[...]
     loop(1, far, small_far_go)
     pass_back(1)
     finalize_all(slots * lper // 2, slots * lper)
     finish(0)
     for t in range(slots):
-        pltpu.make_async_copy(result.at[t], out.at[t], out_sem.at[t]).wait()
+        pltpu.make_async_copy(tile.at[t], out.at[t], out_sem.at[t]).wait()
     finish(1)
     for c in final_copies[:2]:
         c.start()
     loop(1, far, small_far_wait)
-    s = small_far[0]
+    s = small_far[0].astype(F32)
     for p in range(1, far):
-        s = s + small_far[p]
+        s = s + small_far[p].astype(F32)
     write_small(s)
     for c in final_copies[2:]:
         c.start()
@@ -587,17 +597,19 @@
 
 
 def publish_kernel(*refs):
-    n = len(refs) // 2
-    srcs, dsts, sems = refs[:n], refs[n:2 * n], refs[2 * n]
-    copies = []
-    for t in range(srcs[0].shape[0]):
-        copies.append(pltpu.make_async_copy(srcs[0].at[t], dsts[0].at[t], sems.at[len(copies)]))
-    for src, dst in zip(srcs[1:], dsts[1:]):
-        copies.append(pltpu.make_async_copy(src, dst, sems.at[len(copies)]))
-    for c in copies:
+    n = (len(refs) - 1) // 3
+    srcs, dsts, held, sems = refs[:n], refs[n:2 * n], refs[2 * n:3 * n], refs[3 * n]
+    parts = [(srcs[0].at[t], held[0].at[t], dsts[0].at[t]) for t in range(srcs[0].shape[0])]
+    parts += list(zip(srcs[1:], held[1:], dsts[1:]))
+    ins = [pltpu.make_async_copy(src, mid, sems.at[0, i]) for i, (src, mid, _) in enumerate(parts)]
+    outs = [pltpu.make_async_copy(mid, dst, sems.at[1, i]) for i, (_, mid, dst) in enumerate(parts)]
+    for c in ins:
         c.start()
-    for c in copies:
+    for c, d in zip(ins, outs):
         c.wait()
+        d.start()
+    for d in outs:
+        d.wait()
 
 
 def publish(*arrays):
@@ -607,7 +619,8 @@
         in_specs=[anyw] * len(arrays),
         out_specs=[anyw] * len(arrays),
         out_shape=[jax.ShapeDtypeStruct(v.shape, v.dtype) for v in arrays],
-        scratch_shapes=[pltpu.SemaphoreType.DMA((arrays[0].shape[0] + len(arrays) - 1,))],
+        scratch_shapes=[pltpu.VMEM(v.shape, v.dtype) for v in arrays]
+        + [pltpu.SemaphoreType.DMA((2, arrays[0].shape[0] + len(arrays) - 1))],
         compiler_params=pltpu.CompilerParams(vmem_limit_bytes=60 * 2**20),
     )(*arrays)
 
@@ -645,13 +658,12 @@
             v(F32, edge, hh), v(F32, edge, hh), v(F32, edge, hh), v(F32, edge, hh),
             v(BF16, edge, hh), v(BF16, edge, hh), v(BF16, edge, hh), v(BF16, edge, hh),
             v(F32, edge, chans), v(F32, edge, chans), v(F32, LAST_ROWS * width, chans), v(F32, LAST_ROWS * width, chans),
-            v(BF16, *fields.shape),
             v(F32, width * 16, chans), pltpu.SMEM((space,), jnp.int32),
-            v(F32, 2, 2 * chans, hh), v(F32, 13, 8, chans), v(F32, 2, 8, hh), v(F32, 24, chans),
+            v(F32, 2, 2 * chans, hh), v(F32, 13, 8, chans), v(F32, 2, 8, hh), v(BF16, 32, chans),
             v(BF16, 8 * slots, *line), v(BF16, space, *line), v(BF16, space, *line),
             v(BF16, 2, near, *piece), v(BF16, 2, near, *piece), v(BF16, 2, *piece), v(BF16, 2, far, *piece),
             v(BF16, 2, *piece), v(BF16, 2, near, *piece),
-            v(F32, near, 24, chans), v(F32, 24, chans), v(F32, far, 24, chans),
+            v(BF16, near, 32, chans), v(BF16, 32, chans), v(BF16, far, 32, chans), v(F32, 32, chans),
             dma(2, slots), dma(slots), dma(space), dma(space), dma(2, 2, near), dma(2, 2, far), dma(2, 2, near),
             dma(2, near), dma(2, far)],
         compiler_params=pltpu.CompilerParams(

time: 160 us -> 68.6 us (0.43)
  Pallas kernels: 159 us -> 67.9 us
    pallas_call x1, Pallas kernels: 88.8 us -> 2.77 us  [publish(): pl.pallas_call(publish_kernel, in_specs=[anyw] * len(arrays), out_specs=[...]
    pallas_call x1, Pallas kernels: 70.1 us -> 65.1 us  [block(): pl.pallas_call(functools.partial(block_kernel, space, near), in_specs=[an...]
where the time goes in v4:
time: 68.6 us; the launch traced here: 68.5 us
  Pallas kernels  67.9 us (99%)
    pallas_call x1, Pallas kernels, block(): pl.pallas_call(functools.partial(block_kernel, space, near), in_specs=[an...  65.1 us
    pallas_call x1, Pallas kernels, publish(): pl.pallas_call(publish_kernel, in_specs=[anyw] * len(arrays), out_specs=[...  2.77 us

profile of v4, /device:TPU:1, one launch (start us, length us, event | category | flops | bytes accessed | tf_op | source)
XLA Modules:
  0.0 68.5 jit_solution(2109747181274141532)
XLA Ops:
  0.6 65.1 %shard_map.173 = (bf16[4,48,48,128]{3,2,1,0:T(8,128)(2,1)}, f32[128,512]{1,0:T(8,128)}, f32[512,128]{1,0:T(8,128)}, f32[14,128]{1,0:T(8,128)}, f32[1,512]{1,0:T(1,128)}) custom-call(bf16[4,48,48,128]{3,2,1,0:T(8,128)(2,1)} %bitcast.12, bf16[4,48,48,128]{3,2,1,0:T(8,128)(2,1)} %bitcast.13, s32[4,128]{1,0:T(4,128)} %bitcast.14, s32[4,128]{1,0:T(4,128)} %bitcast.15, ...), custom_call_target="tpu_custom_call" | custom-call | tf_op jit(solution)/shard_map/pallas_call | solution.py:641
  65.7 2.8 %shard_map.174 = (bf16[4,48,48,128]{3,2,1,0:T(8,128)(2,1)}, f32[128,512]{1,0:T(8,128)}, f32[512,128]{1,0:T(8,128)}, f32[14,128]{1,0:T(8,128)}, f32[1,512]{1,0:T(1,128)}) custom-call(bf16[4,48,48,128]{3,2,1,0:T(8,128)(2,1)} %get-tuple-element.15.refs_0_, f32[128,512]{1,0:T(8,128)} %get-tuple-element.16.refs_1_, f32[512,128]{1,0:T(8,128)} %get-tuple-element.17.refs_2_, ...), custom_call_target="tpu_custom_call" | custom-call | tf_op jit(solution)/shard_map/pallas_call | solution.py:617

commit v5 on v4

--- a/solution.py
+++ b/solution.py
@@ -54,7 +54,7 @@
 
 def body(space, near, fields, cotangent, nbrs, turns, counts, taps_w, dbias, gain, nbias, bin_, scale, win, bout, wout,
          out, grad_win, grad_wout, channel_out, bias_out, first, final_copies,
-                 tile, cotan, frame, win_t, wout_t, win_h, nhat_s, inv_s, normed_s, branch_s, act_all, dpre_all,
+                 tile, cotan, frame, win_t, half_out, wout_t, win_h, nhat_s, inv_s, normed_s, branch_s, act_all, dpre_all,
                  pre_a, pre_b, dact_a, dact_b, act_a, act_b, dpre_a, dpre_b, proj_b, dnorm_b, rows_a, rows_b,
                  cot_s, codes, grads, sums, bsum, small, cand, outgo, income, halves, got, mid, far_got, spread, whole,
                  small_got, small_mid, small_far, parts,
@@ -100,9 +100,10 @@
     for c in first:
         c.wait()
     win_t[...] = win[...].T
+    half_out[...] = wout[...] * 0.5
     for h in range(2):
         win_h[h] = win[:, h * hh:(h + 1) * hh]
-        wout_t[h] = wout[h * hh:(h + 1) * hh, :].T
+        wout_t[h] = (wout[h * hh:(h + 1) * hh, :] * 0.5).T
     grads[...] = jnp.zeros_like(grads)
     sums[...] = jnp.zeros_like(sums)
     bsum[...] = jnp.zeros_like(bsum)
@@ -198,6 +199,8 @@
         live = jnp.where(t < count, 1.0, 0.0)
         kern = [[taps_w[x, y:y + 1, :] for y in range(3)] for x in range(3)]
         bias = dbias[...]
+        weigh = scale[...] * inner * live
+        s_g = jnp.zeros((8, chans), F32)
         conv = {}
         for fr in range(CONV_ROWS + 2):
             base = (top + fr) * PITCH + 7
@@ -211,11 +214,14 @@
                     conv[r] = acc
             r = fr - 2
             if r >= 0:
+                if r in (0, CONV_ROWS - 1):
+                    ends = weigh * jnp.where((top + r > 0) & (top + r < width - 1), 1.0, 0.0)
                 at = t * area + (top + r) * width
                 norm_rows(conv.pop(r), at)
-                inside = jnp.where((top + r > 0) & (top + r < width - 1), live, 0.0)
-                g = cotan[t, top + r].astype(F32) * inside
-                branch_s[pl.ds(pl.multiple_of(at, 16), width), :] = (g * (scale[...] * inner)).astype(BF16)
+                g = cotan[t, top + r].astype(F32)
+                s_g = s_g + over_rows(g)
+                branch_s[pl.ds(pl.multiple_of(at, 16), width), :] = (g * (ends if r in (0, CONV_ROWS - 1) else weigh)).astype(BF16)
+        sums[12] += s_g * live
 
     loop(0, slots * per, conv_chunk)
 
@@ -295,10 +301,10 @@
         for q in range(0, m, GROUP):
             sl = pl.ds(q, GROUP)
             pre = pre_s[sl, :] + bias
-            ph = 0.5 * lax.erf(pre * (1.0 / math.sqrt(2.0))) + 0.5
-            act_s[sl, :] = (pre * ph).astype(BF16)
-            slope = ph + pre * (jnp.exp(-0.5 * pre * pre) * (1.0 / math.sqrt(2.0 * math.pi)))
-            dpre = dact_s[sl, :] * slope
+            twice = lax.erf(pre * (1.0 / math.sqrt(2.0))) + 1.0
+            act_s[sl, :] = (pre * twice).astype(BF16)
+            bell = jnp.exp2((pre * (-0.5 * math.log2(math.e))) * pre + math.log2(2.0 / math.sqrt(2.0 * math.pi)))
+            dpre = dact_s[sl, :] * (twice + pre * bell)
             bs = bs + over_rows(dpre)
             dpre_s[sl, :] = dpre.astype(BF16)
         bsum[h] += bs
@@ -306,7 +312,8 @@
     def send_near(h):
         prows = 2 * chans // near
         for p in range(near):
-            halves[h, p] = grads[h, p * prows:(p + 1) * prows, :].astype(BF16)
+            part = grads[h, p * prows:(p + 1) * prows, :]
+            halves[h, p] = (part if p < near // 2 else 0.5 * part).astype(BF16)
         got[h, a] = halves[h, a]
 
         def go(o):
@@ -376,16 +383,20 @@
         hidden(k + 1, pre_b, dact_b, act_b, dpre_b)
 
     def stage(i):
-        @pl.when(i == (steps - 3) // 4)
+        @pl.when(i == (steps - 3) // (2 * UNROLL))
         def _():
             if COMM:
                 loop(1, space, halo_wait)
             loop(0, slots, border)
 
         if COMM:
-            @pl.when(i == (steps - 3) // 4 + 1)
+            @pl.when(i == (steps - 3) // (2 * UNROLL) + 1)
             def _():
                 send_near(0)
+
+            @pl.when(i == (steps - 1) // UNROLL - 1)
+            def _():
+                pass_far(0)
 
         for n in range(UNROLL):
             pair(2 + 2 * UNROLL * i + 2 * n)
@@ -395,12 +406,11 @@
     loop(0, (steps - 1) // UNROLL, stage)
     behind(total - 1, act_b, dpre_b)
     if COMM:
-        pass_far(0)
         send_near(1)
     edge_rows = pl.ds(main, m)
     g_proj = jnp.zeros((8, chans), F32)
     for h in range(2):
-        g_proj = g_proj + over_rows(grads[h, chans:2 * chans, :].T * wout[h * hh:(h + 1) * hh, :].astype(F32))
+        g_proj = g_proj + over_rows(grads[h, chans:2 * chans, :].T * half_out[h * hh:(h + 1) * hh, :].astype(F32))
     parts[...] = jnp.zeros_like(parts)
     parts[13:14, :] = jnp.sum(g_proj, axis=0, keepdims=True) / scale[...]
     b = jnp.sum(bsum[...], axis=1)
@@ -466,25 +476,23 @@
     def last(step, rows_s):
         t = step // lper
         top = pl.multiple_of((step - t * lper) * LAST_ROWS, 8)
-        live = jnp.where(t < count, 1.0, 0.0)
         start = pl.multiple_of(t * area + top * width, 16)
         dn = with_border(t, top, rows_s, dnorm_b)
         taps = [[jnp.zeros((8, chans), F32)] * 3 for _ in range(3)]
-        s_g = s_dn = s_dnh = s_dc = jnp.zeros((8, chans), F32)
+        s_dn = s_dnh = s_dc = jnp.zeros((8, chans), F32)
         dconv = {}
         for fr in range(LAST_ROWS + 2):
             r = fr
             if r < LAST_ROWS:
                 sl = pl.ds(pl.multiple_of(start + r * width, 16), width)
-                s_g = s_g + over_rows(cotan[t, top + r].astype(F32))
-                dnorm = dn[r]
+                dnorm = dn[r] * gain[...]
                 nhat = nhat_s[sl, :]
                 dnh = dnorm * nhat
                 s_dn = s_dn + over_rows(dnorm)
                 s_dnh = s_dnh + over_rows(dnh)
-                m1 = jnp.mean(dnorm * gain[...], axis=-1, keepdims=True)
-                m2 = jnp.mean(dnh * gain[...], axis=-1, keepdims=True)
-                dc = inv_s[sl, :] * (dnorm * gain[...] - m1 - nhat * m2)
+                m1 = jnp.mean(dnorm, axis=-1, keepdims=True)
+                m2 = jnp.mean(dnh, axis=-1, keepdims=True)
+                dc = inv_s[sl, :] * (dnorm - m1 - nhat * m2)
                 s_dc = s_dc + over_rows(dc)
                 dconv[r] = dc
             base = (top + fr) * PITCH + 7
@@ -495,7 +503,7 @@
                     for b in range(3):
                         taps[x][b] = taps[x][b] + over_rows(dconv[r] * win3[b])
             dconv.pop(fr - 2, None)
-        for n, s in enumerate([taps[x][b] for x in range(3) for b in range(3)] + [s_dc, s_dnh, s_dn, s_g * live]):
+        for n, s in enumerate([taps[x][b] for x in range(3) for b in range(3)] + [s_dc, s_dnh, s_dn]):
             sums[n] += s
     def finalize(step, rows_s):
         t = step // lper
@@ -516,18 +524,20 @@
         remote(small, small_got.at[a], sn_sem.at[0, o], sn_sem.at[1, a], device).start()
 
     def finalize_all(lo, hi):
-        piped(lo, hi, act_all, wout, finalize)
+        piped(lo, hi, act_all, half_out, finalize)
 
     def between(j):
         if COMM:
             @pl.when(j == slots * lper // 2 * 2 // 3)
             def _():
                 pass_far(1)
+                pass_back(0)
 
     piped(0, slots * lper, dpre_all, win_t, last, between)
 
     tot = jnp.sum(sums[...], axis=1)
-    parts[0:12, :] = tot[0:12]
+    parts[0:10, :] = tot[0:10]
+    parts[10:12, :] = tot[10:12] / gain[...]
     parts[12:13, :] = tot[12:13] * scale[...]
     parts[13:14, :] += tot[12:13] * bout[...]
     small[...] = parts[...].astype(BF16)
@@ -540,13 +550,13 @@
         for n in range(hid // chans):
             bias_out[:, n * chans:(n + 1) * chans] = v[14 + n:15 + n]
 
-    proj_b[...] = jnp.dot(jnp.concatenate([act_all[0, edge_rows, :], act_all[1, edge_rows, :]], axis=1), wout[...],
+    proj_b[...] = jnp.dot(jnp.concatenate([act_all[0, edge_rows, :], act_all[1, edge_rows, :]], axis=1), half_out[...],
                           preferred_element_type=F32)
     if not COMM:
         write_small(parts[...])
         for h in range(2):
             grad_win[:, h * hh:(h + 1) * hh] = grads[h, 0:chans, :]
-            grad_wout[h * hh:(h + 1) * hh, :] = grads[h, chans:2 * chans, :].T
+            grad_wout[h * hh:(h + 1) * hh, :] = 0.5 * grads[h, chans:2 * chans, :].T
         finalize_all(0, slots * lper)
         for c in final_copies:
             c.start()
@@ -568,7 +578,6 @@
         p, device = far_id(far - o)
         remote(small_mid, small_far.at[p], sf_sem.at[0, o], sf_sem.at[1, p], device).wait()
 
-    pass_back(0)
     finalize_all(0, slots * lper // 2)
     loop(1, near, small_near_wait)
     s = small_got[0].astype(F32)
@@ -651,7 +660,7 @@
             v(F32, 1, chans), v(BF16, hid, chans),
             v(F32, chans, hid), v(F32, hid, chans), v(F32, 14, chans), v(F32, 1, hid), dma(12), dma(4),
             v(BF16, *fields.shape), v(BF16, *fields.shape), v(F32, slots, (width + 2) * PITCH + 8, chans),
-            v(BF16, hid, chans), v(BF16, 2, chans, hh), v(BF16, 2, chans, hh),
+            v(BF16, hid, chans), v(BF16, hid, chans), v(BF16, 2, chans, hh), v(BF16, 2, chans, hh),
             v(F32, main + edge, chans), v(F32, main + edge, chans),
             v(BF16, main + edge, chans), v(BF16, main + edge, chans),
             v(BF16, 2, main + edge, hh), v(BF16, 2, main + edge, hh),

time: 68.6 us -> 67.5 us (0.984)
  Pallas kernels: 67.9 us -> 66.7 us
    pallas_call x1, Pallas kernels: 65.1 us -> 64 us  [block(): pl.pallas_call(functools.partial(block_kernel, space, near), in_specs=[an...]
where the time goes in v5:
time: 67.5 us; the launch traced here: 67.4 us
  Pallas kernels  66.7 us (99%)
    pallas_call x1, Pallas kernels, block(): pl.pallas_call(functools.partial(block_kernel, space, near), in_specs=[an...  64 us
    pallas_call x1, Pallas kernels, publish(): pl.pallas_call(publish_kernel, in_specs=[anyw] * len(arrays), out_specs=[...  2.77 us

profile of v5, /device:TPU:1, one launch (start us, length us, event | category | flops | bytes accessed | tf_op | source)
XLA Modules:
  0.0 67.4 jit_solution(8728233106560424947)
XLA Ops:
  0.6 64.0 %shard_map.173 = (bf16[4,48,48,128]{3,2,1,0:T(8,128)(2,1)}, f32[128,512]{1,0:T(8,128)}, f32[512,128]{1,0:T(8,128)}, f32[14,128]{1,0:T(8,128)}, f32[1,512]{1,0:T(1,128)}) custom-call(bf16[4,48,48,128]{3,2,1,0:T(8,128)(2,1)} %bitcast.12, bf16[4,48,48,128]{3,2,1,0:T(8,128)(2,1)} %bitcast.13, s32[4,128]{1,0:T(4,128)} %bitcast.14, s32[4,128]{1,0:T(4,128)} %bitcast.15, ...), custom_call_target="tpu_custom_call" | custom-call | tf_op jit(solution)/shard_map/pallas_call | solution.py:650
  64.6 2.8 %shard_map.174 = (bf16[4,48,48,128]{3,2,1,0:T(8,128)(2,1)}, f32[128,512]{1,0:T(8,128)}, f32[512,128]{1,0:T(8,128)}, f32[14,128]{1,0:T(8,128)}, f32[1,512]{1,0:T(1,128)}) custom-call(bf16[4,48,48,128]{3,2,1,0:T(8,128)(2,1)} %get-tuple-element.15.refs_0_, f32[128,512]{1,0:T(8,128)} %get-tuple-element.16.refs_1_, f32[512,128]{1,0:T(8,128)} %get-tuple-element.17.refs_2_, ...), custom_call_target="tpu_custom_call" | custom-call | tf_op jit(solution)/shard_map/pallas_call | solution.py:626

commit v6 on v5

--- a/solution.py
+++ b/solution.py
@@ -16,6 +16,12 @@
 GROUP = 64
 UNROLL = 2
 COMM = True
+
+
+def settle(pieces, sems, device):
+    copy = remote(pieces, pieces, sems.at[0], sems.at[1], device)
+    copy.wait_send()
+    copy.wait_recv()
 
 
 def over_rows(a):
@@ -58,7 +64,7 @@
                  pre_a, pre_b, dact_a, dact_b, act_a, act_b, dpre_a, dpre_b, proj_b, dnorm_b, rows_a, rows_b,
                  cot_s, codes, grads, sums, bsum, small, cand, outgo, income, halves, got, mid, far_got, spread, whole,
                  small_got, small_mid, small_far, parts,
-                 load_sem, out_sem, halo_send, halo_recv, near_sem, far_sem, back_sem, sn_sem, sf_sem):
+                 load_sem, out_sem, halo_sem, near_sem, far_sem, back_sem, sn_sem, sf_sem):
     slots, width, _, chans = tile.shape
     hid = win.shape[1]
     hh = hid // 2
@@ -116,17 +122,14 @@
         flip = ((turn + (side & 1)) >> 1) & 1
         return flip * picks + 4 * (nbr & (slots - 1)) + edge
 
-    if COMM:
-        def scan(o):
-            peer = lax.rem(me + o, space)
-            hit = jnp.int32(0)
-            for k in range(picks):
-                nbr = nbrs[k & 3, peer * slots + (k >> 2)]
-                hit = jnp.where((nbr >> shift) == me, k, hit)
-            slot = peer * slots + (hit >> 2)
-            codes[o] = pick_code(hit, nbrs[hit & 3, slot], turns[hit & 3, slot])
-
-        loop(0, space, scan)
+    def scan(o):
+        peer = lax.rem(me + o, space)
+        hit = jnp.int32(0)
+        for k in range(picks):
+            nbr = nbrs[k & 3, peer * slots + (k >> 2)]
+            hit = jnp.where((nbr >> shift) == me, k, hit)
+        slot = peer * slots + (hit >> 2)
+        codes[o] = pick_code(hit, nbrs[hit & 3, slot], turns[hit & 3, slot])
 
     def clear(t):
         frame[t, 0:PITCH, :] = jnp.zeros((PITCH, chans), F32)
@@ -137,7 +140,15 @@
             frame[t, pl.ds(pl.multiple_of((r + 1) * PITCH + 8 + width, 8), 8), :] = jnp.zeros((8, chans), F32)
             frame[t, pl.ds(pl.multiple_of((r + 1) * PITCH + 8, 8), width), :] = tile[t, r].astype(F32)
 
-        loop(0, width, side, 4)
+        each = space // slots
+
+        def fill(n):
+            if COMM:
+                scan(t * each + n)
+            for r in range(width // each):
+                side(n * (width // each) + r)
+
+        loop(0, each, fill)
 
     def edge_of(k, q):
         t = k
@@ -173,7 +184,7 @@
         pl.semaphore_wait(barrier, space + near - 2)
 
         loop(1, space, lambda o: remote(
-            outgo.at[o], income.at[me], halo_send.at[o], halo_recv.at[me], (dp, lax.rem(me + o, space))).start())
+            outgo.at[o], income.at[me], halo_sem.at[0], halo_sem.at[1], (dp, lax.rem(me + o, space))).start())
 
     for t in range(slots):
         loads[t][1].wait()
@@ -220,6 +231,8 @@
                 norm_rows(conv.pop(r), at)
                 g = cotan[t, top + r].astype(F32)
                 s_g = s_g + over_rows(g)
+                sides = (t * width + top + r) * 8
+                cot_s[pl.ds(pl.multiple_of(sides, 8), 8), :] = jnp.where(px[0:8] == 0, g[0:8], g[width - 8:width])
                 branch_s[pl.ds(pl.multiple_of(at, 16), width), :] = (g * (ends if r in (0, CONV_ROWS - 1) else weigh)).astype(BF16)
         sums[12] += s_g * live
 
@@ -243,11 +256,6 @@
             else:
                 frame[t, pl.ds(PITCH + 7, width, stride=PITCH), :] = line
 
-        def cots(r):
-            cot_s[pl.ds(pl.multiple_of(r * 16, 8), 8), :] = cotan[t, r, 0:16, :].astype(F32)[0:8]
-            cot_s[pl.ds(pl.multiple_of(r * 16 + 8, 8), 8), :] = cotan[t, r, width - 16:width, :].astype(F32)[8:16]
-
-        loop(0, width, cots, 4)
         for s in range(4):
             acc = dbias[...]
             for x in range(3):
@@ -266,11 +274,11 @@
             if s == 0:
                 g = cotan[t, 0].astype(F32)
             elif s == 1:
-                g = cot_s[pl.ds(15, width, stride=16), :] * inner
+                g = cot_s[pl.ds(t * width * 8 + 7, width, stride=8), :] * inner
             elif s == 2:
                 g = cotan[t, width - 1].astype(F32)
             else:
-                g = cot_s[pl.ds(0, width, stride=16), :] * inner
+                g = cot_s[pl.ds(t * width * 8, width, stride=8), :] * inner
             branch_s[pl.ds(pl.multiple_of(at, 16), width), :] = (g * live * scale[...]).astype(BF16)
 
     steps = (main + slots * 4 * width) // m
@@ -318,16 +326,12 @@
 
         def go(o):
             p, device = near_id(o)
-            remote(halves.at[h, p], got.at[h, a], near_sem.at[h, 0, o], near_sem.at[h, 1, a], device).start()
+            remote(halves.at[h, p], got.at[h, a], near_sem.at[h, 0], near_sem.at[h, 1], device).start()
 
         loop(1, near, go)
 
     def pass_far(h):
-        def wait(o):
-            p, device = near_id(near - o)
-            remote(halves.at[h, p], got.at[h, p], near_sem.at[h, 0, o], near_sem.at[h, 1, p], device).wait()
-
-        loop(1, near, wait)
+        settle(got.at[h, pl.ds(0, near - 1)], near_sem.at[h], near_id(1)[1])
         tot = got[h, 0].astype(F32)
         for p in range(1, near):
             tot = tot + got[h, p].astype(F32)
@@ -336,16 +340,12 @@
 
         def go(o):
             p, device = far_id(o)
-            remote(mid.at[h], far_got.at[h, plane], far_sem.at[h, 0, o], far_sem.at[h, 1, plane], device).start()
+            remote(mid.at[h], far_got.at[h, plane], far_sem.at[h, 0], far_sem.at[h, 1], device).start()
 
         loop(1, far, go)
 
     def pass_back(h):
-        def wait(o):
-            p, device = far_id(far - o)
-            remote(mid.at[h], far_got.at[h, p], far_sem.at[h, 0, o], far_sem.at[h, 1, p], device).wait()
-
-        loop(1, far, wait)
+        settle(far_got.at[h, pl.ds(0, far - 1)], far_sem.at[h], far_id(1)[1])
         tot = far_got[h, 0].astype(F32)
         for p in range(1, far):
             tot = tot + far_got[h, p].astype(F32)
@@ -354,25 +354,17 @@
 
         def go(o):
             p, device = near_id(o)
-            remote(spread.at[h], whole.at[h, a], back_sem.at[h, 0, o], back_sem.at[h, 1, a], device).start()
+            remote(spread.at[h], whole.at[h, a], back_sem.at[h, 0], back_sem.at[h, 1], device).start()
 
         loop(1, near, go)
 
     def finish(h):
-        def wait(o):
-            p, device = near_id(near - o)
-            remote(spread.at[h], whole.at[h, p], back_sem.at[h, 0, o], back_sem.at[h, 1, p], device).wait()
-
-        loop(1, near, wait)
+        settle(whole.at[h, pl.ds(0, near - 1)], back_sem.at[h], near_id(1)[1])
         prows = 2 * chans // near
         hs = slice(h * hh, (h + 1) * hh)
         full = whole[h].reshape(2 * chans, hh).astype(F32)
         grad_win[:, hs] = full[:chans]
         grad_wout[hs, :] = full[chans:].T
-
-    def halo_wait(o):
-        src = lax.rem(me + space - o, space)
-        remote(outgo.at[o], income.at[src], halo_send.at[o], halo_recv.at[src], (dp, src)).wait()
 
     def pair(k):
         behind(jnp.maximum(k - 1, 0), act_b, dpre_b)
@@ -386,7 +378,7 @@
         @pl.when(i == (steps - 3) // (2 * UNROLL))
         def _():
             if COMM:
-                loop(1, space, halo_wait)
+                settle(income.at[pl.ds(0, space - 1)], halo_sem, (dp, lax.rem(me + 1, space)))
             loop(0, slots, border)
 
         if COMM:
@@ -521,7 +513,7 @@
 
     def small_near(o):
         p, device = near_id(o)
-        remote(small, small_got.at[a], sn_sem.at[0, o], sn_sem.at[1, a], device).start()
+        remote(small, small_got.at[a], sn_sem.at[0], sn_sem.at[1], device).start()
 
     def finalize_all(lo, hi):
         piped(lo, hi, act_all, half_out, finalize)
@@ -566,20 +558,12 @@
             c.wait()
         return
 
-    def small_near_wait(o):
-        p, device = near_id(near - o)
-        remote(small, small_got.at[p], sn_sem.at[0, o], sn_sem.at[1, p], device).wait()
-
     def small_far_go(o):
         p, device = far_id(o)
-        remote(small_mid, small_far.at[plane], sf_sem.at[0, o], sf_sem.at[1, plane], device).start()
-
-    def small_far_wait(o):
-        p, device = far_id(far - o)
-        remote(small_mid, small_far.at[p], sf_sem.at[0, o], sf_sem.at[1, p], device).wait()
+        remote(small_mid, small_far.at[plane], sf_sem.at[0], sf_sem.at[1], device).start()
 
     finalize_all(0, slots * lper // 2)
-    loop(1, near, small_near_wait)
+    settle(small_got.at[pl.ds(0, near - 1)], sn_sem, near_id(1)[1])
     s = small_got[0].astype(F32)
     for p in range(1, near):
         s = s + small_got[p].astype(F32)
@@ -594,7 +578,7 @@
     finish(1)
     for c in final_copies[:2]:
         c.start()
-    loop(1, far, small_far_wait)
+    settle(small_far.at[pl.ds(0, far - 1)], sf_sem, far_id(1)[1])
     s = small_far[0].astype(F32)
     for p in range(1, far):
         s = s + small_far[p].astype(F32)
@@ -667,16 +651,15 @@
             v(F32, edge, hh), v(F32, edge, hh), v(F32, edge, hh), v(F32, edge, hh),
             v(BF16, edge, hh), v(BF16, edge, hh), v(BF16, edge, hh), v(BF16, edge, hh),
             v(F32, edge, chans), v(F32, edge, chans), v(F32, LAST_ROWS * width, chans), v(F32, LAST_ROWS * width, chans),
-            v(F32, width * 16, chans), pltpu.SMEM((space,), jnp.int32),
+            v(F32, slots * width * 8, chans), pltpu.SMEM((space,), jnp.int32),
             v(F32, 2, 2 * chans, hh), v(F32, 13, 8, chans), v(F32, 2, 8, hh), v(BF16, 32, chans),
             v(BF16, 8 * slots, *line), v(BF16, space, *line), v(BF16, space, *line),
             v(BF16, 2, near, *piece), v(BF16, 2, near, *piece), v(BF16, 2, *piece), v(BF16, 2, far, *piece),
             v(BF16, 2, *piece), v(BF16, 2, near, *piece),
             v(BF16, near, 32, chans), v(BF16, 32, chans), v(BF16, far, 32, chans), v(F32, 32, chans),
-            dma(2, slots), dma(slots), dma(space), dma(space), dma(2, 2, near), dma(2, 2, far), dma(2, 2, near),
-            dma(2, near), dma(2, far)],
+            dma(2, slots), dma(slots), dma(2), dma(2, 2), dma(2, 2), dma(2, 2), dma(2), dma(2)],
         compiler_params=pltpu.CompilerParams(
-            vmem_limit_bytes=60 * 2**20, **(dict(collective_id=0, has_side_effects=True) if COMM else {})),
+            vmem_limit_bytes=61 * 2**20, **(dict(collective_id=0, has_side_effects=True) if COMM else {})),
     )(fields, cotan, nbrs, turns, counts, kern, row(dbias), row(gain), row(nbias), bin_.reshape(2, 1, hh), row(scale),
       win, row(bout), wout)
 

time: 67.5 us -> 62.1 us (0.920)
  Pallas kernels: 66.7 us -> 61.3 us
    pallas_call x1, Pallas kernels: 64 us -> 58.6 us  [block(): pl.pallas_call(functools.partial(block_kernel, space, near), in_specs=[an...]
where the time goes in v6:
time: 62.1 us; the launch traced here: 62 us
  Pallas kernels  61.3 us (99%)
  between operations  0.65 us (1%)
    pallas_call x1, Pallas kernels, block(): pl.pallas_call(functools.partial(block_kernel, space, near), in_specs=[an...  58.6 us
    pallas_call x1, Pallas kernels, publish(): pl.pallas_call(publish_kernel, in_specs=[anyw] * len(arrays), out_specs=[...  2.77 us

profile of v6, /device:TPU:1, one launch (start us, length us, event | category | flops | bytes accessed | tf_op | source)
XLA Modules:
  0.0 62.0 jit_solution(442365347871686718)
XLA Ops:
  0.6 58.6 %shard_map.173 = (bf16[4,48,48,128]{3,2,1,0:T(8,128)(2,1)}, f32[128,512]{1,0:T(8,128)}, f32[512,128]{1,0:T(8,128)}, f32[14,128]{1,0:T(8,128)}, f32[1,512]{1,0:T(1,128)}) custom-call(bf16[4,48,48,128]{3,2,1,0:T(8,128)(2,1)} %bitcast.12, bf16[4,48,48,128]{3,2,1,0:T(8,128)(2,1)} %bitcast.13, s32[4,128]{1,0:T(4,128)} %bitcast.14, s32[4,128]{1,0:T(4,128)} %bitcast.15, ...), custom_call_target="tpu_custom_call" | custom-call | tf_op jit(solution)/shard_map/pallas_call | solution.py:634
  59.2 2.8 %shard_map.174 = (bf16[4,48,48,128]{3,2,1,0:T(8,128)(2,1)}, f32[128,512]{1,0:T(8,128)}, f32[512,128]{1,0:T(8,128)}, f32[14,128]{1,0:T(8,128)}, f32[1,512]{1,0:T(1,128)}) custom-call(bf16[4,48,48,128]{3,2,1,0:T(8,128)(2,1)} %get-tuple-element.15.refs_0_, f32[128,512]{1,0:T(8,128)} %get-tuple-element.16.refs_1_, f32[512,128]{1,0:T(8,128)} %get-tuple-element.17.refs_2_, ...), custom_call_target="tpu_custom_call" | custom-call | tf_op jit(solution)/shard_map/pallas_call | solution.py:610

commit v7 on v6

--- a/solution.py
+++ b/solution.py
@@ -11,7 +11,7 @@
 F32, BF16 = jnp.float32, jnp.bfloat16
 MESH = pl.DeviceIdType.MESH
 PITCH = 64
-CONV_ROWS = 16
+CONV_ROWS = 12
 LAST_ROWS = 16
 GROUP = 64
 UNROLL = 2
@@ -592,7 +592,10 @@
 def publish_kernel(*refs):
     n = (len(refs) - 1) // 3
     srcs, dsts, held, sems = refs[:n], refs[n:2 * n], refs[2 * n:3 * n], refs[3 * n]
-    parts = [(srcs[0].at[t], held[0].at[t], dsts[0].at[t]) for t in range(srcs[0].shape[0])]
+    slots, width = srcs[0].shape[:2]
+    third = width // 3
+    cuts = [(t, pl.ds(r, third)) for t in range(slots) for r in range(0, width, third)]
+    parts = [tuple(ref.at[t, r] for ref in (srcs[0], held[0], dsts[0])) for t, r in cuts]
     parts += list(zip(srcs[1:], held[1:], dsts[1:]))
     ins = [pltpu.make_async_copy(src, mid, sems.at[0, i]) for i, (src, mid, _) in enumerate(parts)]
     outs = [pltpu.make_async_copy(mid, dst, sems.at[1, i]) for i, (_, mid, dst) in enumerate(parts)]
@@ -613,7 +616,7 @@
         out_specs=[anyw] * len(arrays),
         out_shape=[jax.ShapeDtypeStruct(v.shape, v.dtype) for v in arrays],
         scratch_shapes=[pltpu.VMEM(v.shape, v.dtype) for v in arrays]
-        + [pltpu.SemaphoreType.DMA((2, arrays[0].shape[0] + len(arrays) - 1))],
+        + [pltpu.SemaphoreType.DMA((2, 3 * arrays[0].shape[0] + len(arrays) - 1))],
         compiler_params=pltpu.CompilerParams(vmem_limit_bytes=60 * 2**20),
     )(*arrays)
 

time: 62.1 us -> 62.1 us (level)
  no operation moved by 1% of the time
where the time goes in v7:
time: 62.1 us; the launch traced here: 61.9 us
  Pallas kernels  61.3 us (99%)
  between operations  0.65 us (1%)
    pallas_call x1, Pallas kernels, block(): pl.pallas_call(functools.partial(block_kernel, space, near), in_specs=[an...  58.4 us
    pallas_call x1, Pallas kernels, publish(): pl.pallas_call(publish_kernel, in_specs=[anyw] * len(arrays), out_specs=[...  2.92 us

profile of v7, /device:TPU:1, one launch (start us, length us, event | category | flops | bytes accessed | tf_op | source)
XLA Modules:
  0.0 61.9 jit_solution(5600522937063534508)
XLA Ops:
  0.6 58.4 %shard_map.173 = (bf16[4,48,48,128]{3,2,1,0:T(8,128)(2,1)}, f32[128,512]{1,0:T(8,128)}, f32[512,128]{1,0:T(8,128)}, f32[14,128]{1,0:T(8,128)}, f32[1,512]{1,0:T(1,128)}) custom-call(bf16[4,48,48,128]{3,2,1,0:T(8,128)(2,1)} %bitcast.12, bf16[4,48,48,128]{3,2,1,0:T(8,128)(2,1)} %bitcast.13, s32[4,128]{1,0:T(4,128)} %bitcast.14, s32[4,128]{1,0:T(4,128)} %bitcast.15, ...), custom_call_target="tpu_custom_call" | custom-call | tf_op jit(solution)/shard_map/pallas_call | solution.py:637
  59.0 2.9 %shard_map.174 = (bf16[4,48,48,128]{3,2,1,0:T(8,128)(2,1)}, f32[128,512]{1,0:T(8,128)}, f32[512,128]{1,0:T(8,128)}, f32[14,128]{1,0:T(8,128)}, f32[1,512]{1,0:T(1,128)}) custom-call(bf16[4,48,48,128]{3,2,1,0:T(8,128)(2,1)} %get-tuple-element.15.refs_0_, f32[128,512]{1,0:T(8,128)} %get-tuple-element.16.refs_1_, f32[512,128]{1,0:T(8,128)} %get-tuple-element.17.refs_2_, ...), custom_call_target="tpu_custom_call" | custom-call | tf_op jit(solution)/shard_map/pallas_call | solution.py:613
